TPU v7x, 32 devices: a whole 2x2x4 slice. The times are simulated.
32 devices in a mesh: seq: 8 (over y, x, core), tp: 4 (over z).
Axes of the slice: x: 2, y: 2, z: 4, core: 2. Of those that a mesh axis runs over, the one named last changes fastest.
Arguments:
- patches: bfloat16 [4096, 1152], P(('seq', 'tp')), may hold values from -6 to 6
- image_patches: int32 [8], P('seq'), may hold values from 385 to 512, as said below
- attn_norm_gain: float32 [1152], replicated, may hold values from 0.1 to 1.9
- attn_norm_shift: float32 [1152], replicated, may hold values from -3 to 3
- query_weight: bfloat16 [1152, 1152], P('seq', 'tp'), may hold values from -0.1875 to 0.1875
- query_bias: float32 [1152], P('tp'), may hold values from -3 to 3
- key_weight: bfloat16 [1152, 1152], P('seq', 'tp'), may hold values from -0.1875 to 0.1875
- value_weight: bfloat16 [1152, 1152], P('seq', 'tp'), may hold values from -0.1875 to 0.1875
- value_bias: float32 [1152], P('tp'), may hold values from -3 to 3
- out_weight: bfloat16 [1152, 1152], P('tp', 'seq'), may hold values from -1 to 1
- out_bias: float32 [1152], replicated, may hold values from -3 to 3
- mlp_norm_gain: float32 [1152], replicated, may hold values from 0.1 to 1.9
- mlp_norm_shift: float32 [1152], replicated, may hold values from -3 to 3
- fc_in_weight: bfloat16 [1152, 4304], P('seq', 'tp'), may hold values from -0.1875 to 0.1875
- fc_in_bias: float32 [4304], P('tp'), may hold values from -3 to 3
- fc_out_weight: bfloat16 [4304, 1152], P('tp', 'seq'), may hold values from -0.125 to 0.125
- fc_out_bias: float32 [1152], replicated, may hold values from -3 to 3
- proj_gate: bfloat16 [1152, 14336], P('seq', 'tp'), may hold values from -0.1875 to 0.1875
- proj_up: bfloat16 [1152, 14336], P('seq', 'tp'), may hold values from -0.1875 to 0.1875
- proj_down: bfloat16 [4096, 14336], P('seq', 'tp'), may hold values from -0.09375 to 0.09375
- latent_param: bfloat16 [64, 4096], P('tp', 'seq'), may hold values from -6 to 6
- context_gain: float32 [4096], replicated, may hold values from 0.1 to 1.9
- latent_gain: float32 [4096], replicated, may hold values from 0.1 to 1.9
- res_query: bfloat16 [4096, 1536], P('seq', 'tp'), may hold values from -0.09375 to 0.09375
- res_key: bfloat16 [4096, 384], P('seq', 'tp'), may hold values from -0.09375 to 0.09375
- res_value: bfloat16 [4096, 384], P('seq', 'tp'), may hold values from -0.09375 to 0.09375
- res_out: bfloat16 [1536, 4096], P('tp', 'seq'), may hold values from -1 to 1
- post_gain: float32 [4096], replicated, may hold values from 0.1 to 1.9
- ffn_gate: bfloat16 [16384, 4096], P(('seq', 'tp')), may hold values from -0.09375 to 0.09375
- ffn_up: bfloat16 [16384, 4096], P(('seq', 'tp')), may hold values from -0.09375 to 0.09375
- ffn_down: bfloat16 [16384, 4096], P(('seq', 'tp')), may hold values from -0.09375 to 0.09375
- cotangent: bfloat16 [512, 4096], P(('seq', 'tp')), may hold values from -6 to 6
Outputs:
- latents: bfloat16 [512, 4096], P(('seq', 'tp'))
- patches_grad: float32 [4096, 1152], P(('seq', 'tp'))
- grad_attn_norm_gain: float32 [1152], replicated
- grad_attn_norm_shift: float32 [1152], replicated
- grad_query_weight: float32 [1152, 1152], P('seq', 'tp')
- grad_query_bias: float32 [1152], P('tp')
- grad_key_weight: float32 [1152, 1152], P('seq', 'tp')
- grad_value_weight: float32 [1152, 1152], P('seq', 'tp')
- grad_value_bias: float32 [1152], P('tp')
- grad_out_weight: float32 [1152, 1152], P('tp', 'seq')
- grad_out_bias: float32 [1152], replicated
- grad_mlp_norm_gain: float32 [1152], replicated
- grad_mlp_norm_shift: float32 [1152], replicated
- grad_fc_in_weight: float32 [1152, 4304], P('seq', 'tp')
- grad_fc_in_bias: float32 [4304], P('tp')
- grad_fc_out_weight: float32 [4304, 1152], P('tp', 'seq')
- grad_fc_out_bias: float32 [1152], replicated
- grad_proj_gate: float32 [1152, 14336], P('seq', 'tp')
- grad_proj_up: float32 [1152, 14336], P('seq', 'tp')
- grad_proj_down: float32 [4096, 14336], P('seq', 'tp')
- grad_latent_param: float32 [64, 4096], P('tp', 'seq')
- grad_context_gain: float32 [4096], replicated
- grad_latent_gain: float32 [4096], replicated
- grad_res_query: float32 [4096, 1536], P('seq', 'tp')
- grad_res_key: float32 [4096, 384], P('seq', 'tp')
- grad_res_value: float32 [4096, 384], P('seq', 'tp')
- grad_res_out: float32 [1536, 4096], P('tp', 'seq')
- grad_post_gain: float32 [4096], replicated
- grad_ffn_gate: float32 [16384, 4096], P(('seq', 'tp'))
- grad_ffn_up: float32 [16384, 4096], P(('seq', 'tp'))
- grad_ffn_down: float32 [16384, 4096], P(('seq', 'tp'))
Inputs may be any that keep to these rules, and one draw needn't show every extreme that they name: `image_patches`: valid patches of each image fill its first slots; every image holds more than three quarters of its 512 slots, and some image holds all 512.
All inputs are finite; a program needn't handle non-finite values.
Results may differ from a plain program's by a relative error of at most 0.03.
Values may be sent and summed in bfloat16 or wider, within the bound.
No kernel may reach another device: no remote copies, remote signals or barrier semaphores. Data moves between devices by JAX's collectives and lax.ppermute only.
A program may use at most 640 MiB of HBM per device.

v0:
```python
import jax
import jax.numpy as jnp
from jax import lax
from jax.sharding import PartitionSpec as P

HD_V = 72
H_R = 16
KV_R = 4
HD_R = 96


eps_norm = 1e-06
masked_out = -1e30


def as_sent(value):
    return jax.tree.map(lambda a: a.astype(jnp.bfloat16) if a.dtype == jnp.float32 else a, value)


def layer_norm(inputs, norm_gain, norm_shift):
    row_mean = jnp.mean(inputs, axis=-1, keepdims=True)
    centered = inputs - row_mean
    row_var = jnp.mean(centered * centered, axis=-1, keepdims=True)
    return centered * lax.rsqrt(row_var + eps_norm) * norm_gain + norm_shift


def rms_norm(inputs, norm_gain):
    return (
        inputs * lax.rsqrt(jnp.mean(inputs * inputs, axis=-1, keepdims=True) + eps_norm) * norm_gain
    )


def gelu_tanh(inputs):
    return jax.nn.gelu(inputs, approximate=True)


def swish_gate(gate_pre, up_pre):
    return jax.nn.silu(gate_pre) * up_pre


def swish_back(gate_pre, up_pre, grad_hidden):
    ignored, pull_back = jax.vjp(swish_gate, gate_pre, up_pre)
    grad_gate, grad_up = pull_back(grad_hidden)
    return (grad_gate.astype(jnp.bfloat16), grad_up.astype(jnp.bfloat16))


def times_plain(left_side, right_side):
    return jnp.dot(left_side, right_side, preferred_element_type=jnp.float32)


def times_left(left_side, right_side):
    return lax.dot_general(
        left_side, right_side, (((0,), (0,)), ((), ())), preferred_element_type=jnp.float32
    )


def times_right(left_side, right_side):
    return lax.dot_general(
        left_side, right_side, (((1,), (1,)), ((), ())), preferred_element_type=jnp.float32
    )


def attend(query_rows, key_rows, value_rows, valid_keys, score_scale):
    scores = (
        jnp.einsum("qcge,kce->cgqk", query_rows, key_rows, preferred_element_type=jnp.float32)
        * score_scale
    )
    scores = jnp.where(valid_keys, scores, masked_out)
    top_score = jnp.max(scores, axis=-1, keepdims=True)
    total = jnp.sum(jnp.exp(scores - top_score), axis=-1, keepdims=True)
    log_total = top_score + jnp.log(total)
    weights = jnp.exp(scores - log_total).astype(jnp.bfloat16)
    mixed_rows = jnp.einsum(
        "cgqk,kce->qcge", weights, value_rows, preferred_element_type=jnp.float32
    )
    return (mixed_rows.astype(jnp.bfloat16), log_total)


def attend_back(query_rows, key_rows, value_rows, valid_keys, score_scale, log_total, grad_mixed):
    scores = (
        jnp.einsum("qcge,kce->cgqk", query_rows, key_rows, preferred_element_type=jnp.float32)
        * score_scale
    )
    scores = jnp.where(valid_keys, scores, masked_out)
    probs_full = jnp.exp(scores - log_total)
    grad_probs = jnp.einsum(
        "qcge,kce->cgqk", grad_mixed, value_rows, preferred_element_type=jnp.float32
    )
    inner_sum = jnp.sum(probs_full * grad_probs, axis=-1, keepdims=True)
    grad_scores = (probs_full * (grad_probs - inner_sum)).astype(jnp.bfloat16)
    grad_query = (
        jnp.einsum("cgqk,kce->qcge", grad_scores, key_rows, preferred_element_type=jnp.float32)
        * score_scale
    ).astype(jnp.bfloat16)
    grad_key = (
        jnp.einsum("cgqk,qcge->kce", grad_scores, query_rows, preferred_element_type=jnp.float32)
        * score_scale
    ).astype(jnp.bfloat16)
    grad_value = jnp.einsum(
        "cgqk,qcge->kce",
        probs_full.astype(jnp.bfloat16),
        grad_mixed,
        preferred_element_type=jnp.float32,
    ).astype(jnp.bfloat16)
    return (grad_query, grad_key, grad_value)


def gather_narrow(rows_in):
    return lax.all_gather(rows_in, "tp", axis=0, tiled=True)


def sum_narrow(terms):
    return lax.psum_scatter(
        terms.astype(jnp.bfloat16), "tp", scatter_dimension=0, tiled=True
    ).astype(jnp.float32)


def gather_wide(rows_in):
    return jax.tree.map(
        lambda part, own: part.astype(own.dtype),
        lax.all_gather(as_sent(rows_in), "tp", axis=0, tiled=True),
        rows_in,
    )


def sum_wide(terms):
    return jax.tree.map(
        lambda part: part.astype(jnp.float32),
        lax.psum_scatter(as_sent(terms), "tp", scatter_dimension=0, tiled=True),
    )


def fetch_vision(query_weight, key_weight, value_weight, out_weight, fc_in_weight, fc_out_weight):
    return (
        lax.all_gather(query_weight, "seq", axis=0, tiled=True),
        lax.all_gather(key_weight, "seq", axis=0, tiled=True),
        lax.all_gather(value_weight, "seq", axis=0, tiled=True),
        lax.all_gather(out_weight, "seq", axis=1, tiled=True),
        lax.all_gather(fc_in_weight, "seq", axis=0, tiled=True),
        lax.all_gather(fc_out_weight, "seq", axis=1, tiled=True),
    )


def fetch_projection(proj_gate, proj_up, proj_down):
    return (
        lax.all_gather(proj_gate, "seq", axis=0, tiled=True),
        lax.all_gather(proj_up, "seq", axis=0, tiled=True),
        lax.all_gather(proj_down, "seq", axis=0, tiled=True),
    )


def fetch_resampler(latent_param, res_query, res_key, res_value, res_out):
    return (
        lax.all_gather(latent_param, "seq", axis=1, tiled=True),
        lax.all_gather(res_query, "seq", axis=0, tiled=True),
        lax.all_gather(res_key, "seq", axis=0, tiled=True),
        lax.all_gather(res_value, "seq", axis=0, tiled=True),
        lax.all_gather(res_out, "seq", axis=1, tiled=True),
    )


def fetch_ffn(ffn_gate, ffn_up, ffn_down):
    return (
        lax.all_gather(ffn_gate, "seq", axis=0, tiled=True),
        lax.all_gather(ffn_up, "seq", axis=0, tiled=True),
        lax.all_gather(ffn_down, "seq", axis=0, tiled=True),
    )


def spread_slot(vector, tensor, tp_index):
    whole_vec = jnp.zeros((vector.shape[0] * tensor,), jnp.float32)
    return lax.dynamic_update_slice_in_dim(whole_vec, vector, tp_index * vector.shape[0], 0)


def take_slot(vector, tensor, tp_index):
    slot_width = vector.shape[0] // tensor
    return lax.dynamic_slice_in_dim(vector, tp_index * slot_width, slot_width, 0)


def shards(
    patches,
    image_patches,
    attn_norm_gain,
    attn_norm_shift,
    query_weight,
    query_bias,
    key_weight,
    value_weight,
    value_bias,
    out_weight,
    out_bias,
    mlp_norm_gain,
    mlp_norm_shift,
    fc_in_weight,
    fc_in_bias,
    fc_out_weight,
    fc_out_bias,
    proj_gate,
    proj_up,
    proj_down,
    latent_param,
    context_gain,
    latent_gain,
    res_query,
    res_key,
    res_value,
    res_out,
    post_gain,
    ffn_gate,
    ffn_up,
    ffn_down,
    cotangent,
):
    tensor = lax.axis_size("tp")
    tp_index = lax.axis_index("tp")
    patch_rows = patches.astype(jnp.float32)
    seq_len = patches.shape[0] * tensor
    image_count = image_patches[0]
    row_valid = jnp.arange(seq_len) < image_count
    vis_valid = row_valid[None, None, None, :]
    vis_heads = query_weight.shape[1] // HD_V
    kv_local = res_key.shape[1] // HD_R
    group_size = H_R // KV_R
    vis_scale = HD_V ** (-0.5)
    res_scale = HD_R ** (-0.5)
    vis_fwd = fetch_vision(
        query_weight, key_weight, value_weight, out_weight, fc_in_weight, fc_out_weight
    )
    query_full, key_full, value_full, out_full, fc_in_full, fc_out_full = vis_fwd
    norm_one = layer_norm(patch_rows, attn_norm_gain, attn_norm_shift).astype(jnp.bfloat16)
    norm_all = gather_narrow(norm_one)
    query_rows = (
        (times_plain(norm_all, query_full) + query_bias)
        .astype(jnp.bfloat16)
        .reshape(seq_len, vis_heads, 1, HD_V)
    )
    key_rows = (
        times_plain(norm_all, key_full).astype(jnp.bfloat16).reshape(seq_len, vis_heads, HD_V)
    )
    value_rows = (
        (times_plain(norm_all, value_full) + value_bias)
        .astype(jnp.bfloat16)
        .reshape(seq_len, vis_heads, HD_V)
    )
    attended, vis_total = attend(query_rows, key_rows, value_rows, vis_valid, vis_scale)
    attended = attended.reshape(seq_len, vis_heads * HD_V)
    after_attn = patch_rows + sum_narrow(times_plain(attended, out_full)) + out_bias
    norm_two = layer_norm(after_attn, mlp_norm_gain, mlp_norm_shift).astype(jnp.bfloat16)
    norm_two_all = gather_narrow(norm_two)
    fc_pre = times_plain(norm_two_all, fc_in_full) + fc_in_bias
    fc_act = gelu_tanh(fc_pre).astype(jnp.bfloat16)
    vis_out = after_attn + sum_narrow(times_plain(fc_act, fc_out_full)) + fc_out_bias
    proj_fwd = fetch_projection(proj_gate, proj_up, proj_down)
    pgate_full, pup_full, pdown_full = proj_fwd
    vis_all = gather_narrow(vis_out.astype(jnp.bfloat16))
    gate_pre = times_plain(vis_all, pgate_full)
    up_pre = times_plain(vis_all, pup_full)
    hidden = swish_gate(gate_pre, up_pre).astype(jnp.bfloat16)
    context = sum_wide(times_right(hidden, pdown_full))
    res_fwd = fetch_resampler(latent_param, res_query, res_key, res_value, res_out)
    lat_full, rq_full, rk_full, rv_full, ro_full = res_fwd
    lat_rows = lat_full.astype(jnp.float32)
    ctx_norm = rms_norm(context, context_gain).astype(jnp.bfloat16)
    lat_norm = rms_norm(lat_rows, latent_gain).astype(jnp.bfloat16)
    ctx_all, lat_all = gather_wide((ctx_norm, lat_norm))
    kv_input = jnp.concatenate([ctx_all, lat_all], axis=0)
    latent_count = lat_all.shape[0]
    res_valid = jnp.concatenate([row_valid, jnp.ones((latent_count,), jnp.bool_)])[
        None, None, None, :
    ]
    res_queries = (
        times_plain(lat_all, rq_full)
        .astype(jnp.bfloat16)
        .reshape(latent_count, kv_local, group_size, HD_R)
    )
    res_keys = (
        times_plain(kv_input, rk_full)
        .astype(jnp.bfloat16)
        .reshape(kv_input.shape[0], kv_local, HD_R)
    )
    res_values = (
        times_plain(kv_input, rv_full)
        .astype(jnp.bfloat16)
        .reshape(kv_input.shape[0], kv_local, HD_R)
    )
    res_mixed, res_total = attend(res_queries, res_keys, res_values, res_valid, res_scale)
    res_mixed = res_mixed.reshape(latent_count, kv_local * group_size * HD_R)
    lat_after = lat_rows + sum_wide(times_plain(res_mixed, ro_full))
    post_norm = rms_norm(lat_after, post_gain).astype(jnp.bfloat16)
    ffn_fwd = fetch_ffn(ffn_gate, ffn_up, ffn_down)
    fgate_full, fup_full, fdown_full = ffn_fwd
    ffn_input = gather_wide(post_norm)
    ffn_gate_pre = times_right(ffn_input, fgate_full)
    ffn_up_pre = times_right(ffn_input, fup_full)
    ffn_hidden = swish_gate(ffn_gate_pre, ffn_up_pre).astype(jnp.bfloat16)
    ffn_out = sum_wide(times_plain(ffn_hidden, fdown_full))
    latents = (lat_after + ffn_out).astype(jnp.bfloat16)
    grad_out = cotangent.astype(jnp.float32)
    ffn_back = fetch_ffn(ffn_gate, ffn_up, ffn_down)
    fgate_back, fup_back, fdown_back = ffn_back
    grad_every = gather_wide(cotangent)
    grad_down_full = times_left(ffn_hidden, grad_every)
    grad_fhidden = times_right(grad_every, fdown_back)
    grad_fgate, grad_fup = swish_back(ffn_gate_pre, ffn_up_pre, grad_fhidden)
    grad_gate_full = times_left(grad_fgate, ffn_input)
    grad_up_full = times_left(grad_fup, ffn_input)
    grad_post = sum_wide(times_plain(grad_fgate, fgate_back) + times_plain(grad_fup, fup_back))
    grad_ffn_gate, grad_ffn_up, grad_ffn_down = (
        lax.psum_scatter(grad_gate_full, "seq", scatter_dimension=0, tiled=True),
        lax.psum_scatter(grad_up_full, "seq", scatter_dimension=0, tiled=True),
        lax.psum_scatter(grad_down_full, "seq", scatter_dimension=0, tiled=True),
    )
    ignored, pull_post = jax.vjp(rms_norm, lat_after, post_gain)
    grad_lat_post, grad_post_gain = pull_post(grad_post)
    grad_after = grad_out + grad_lat_post
    res_back = fetch_resampler(latent_param, res_query, res_key, res_value, res_out)
    grad_after_all = gather_wide(grad_after.astype(jnp.bfloat16))
    grad_ro_full = times_left(res_mixed, grad_after_all)
    grad_rmixed = (
        times_right(grad_after_all, res_back[4])
        .astype(jnp.bfloat16)
        .reshape(latent_count, kv_local, group_size, HD_R)
    )
    grad_rq, grad_rk, grad_rv = attend_back(
        res_queries, res_keys, res_values, res_valid, res_scale, res_total, grad_rmixed
    )
    grad_rq = grad_rq.reshape(latent_count, kv_local * group_size * HD_R)
    grad_rk = grad_rk.reshape(kv_input.shape[0], kv_local * HD_R)
    grad_rv = grad_rv.reshape(kv_input.shape[0], kv_local * HD_R)
    grad_rq_full = times_left(lat_all, grad_rq)
    grad_rk_full = times_left(kv_input, grad_rk)
    grad_rv_full = times_left(kv_input, grad_rv)
    grad_kv = times_right(grad_rk, res_back[2]) + times_right(grad_rv, res_back[3])
    grad_lat_part = times_right(grad_rq, res_back[1]) + grad_kv[seq_len:]
    grad_ctx_norm, grad_lat_norm = sum_wide((grad_kv[:seq_len], grad_lat_part))
    ignored, pull_ctx = jax.vjp(rms_norm, context, context_gain)
    grad_context, grad_context_gain = pull_ctx(grad_ctx_norm)
    ignored, pull_lat = jax.vjp(rms_norm, lat_rows, latent_gain)
    grad_lat_rows, grad_latent_gain = pull_lat(grad_lat_norm)
    grad_latent_param, grad_res_query, grad_res_key, grad_res_value, grad_res_out = (
        lax.psum_scatter(grad_after + grad_lat_rows, "seq", scatter_dimension=1, tiled=True),
        lax.psum_scatter(grad_rq_full, "seq", scatter_dimension=0, tiled=True),
        lax.psum_scatter(grad_rk_full, "seq", scatter_dimension=0, tiled=True),
        lax.psum_scatter(grad_rv_full, "seq", scatter_dimension=0, tiled=True),
        lax.psum_scatter(grad_ro_full, "seq", scatter_dimension=1, tiled=True),
    )
    grad_ctx_all = gather_wide(grad_context.astype(jnp.bfloat16))
    proj_back = fetch_projection(proj_gate, proj_up, proj_down)
    grad_pdown_full = times_left(grad_ctx_all, hidden)
    grad_phidden = times_plain(grad_ctx_all, proj_back[2])
    grad_pgate, grad_pup = swish_back(gate_pre, up_pre, grad_phidden)
    grad_pgate_full = times_left(vis_all, grad_pgate)
    grad_pup_full = times_left(vis_all, grad_pup)
    grad_vis = sum_narrow(
        times_right(grad_pgate, proj_back[0]) + times_right(grad_pup, proj_back[1])
    )
    vis_back = fetch_vision(
        query_weight, key_weight, value_weight, out_weight, fc_in_weight, fc_out_weight
    )
    grad_fc_out_rows = jnp.sum(grad_vis, axis=0)
    grad_vis_all = gather_narrow(grad_vis.astype(jnp.bfloat16))
    grad_fc_out_full = times_left(fc_act, grad_vis_all)
    grad_act = times_right(grad_vis_all, vis_back[5])
    ignored, pull_gelu = jax.vjp(gelu_tanh, fc_pre)
    grad_fc_pre = pull_gelu(grad_act)[0].astype(jnp.bfloat16)
    grad_fc_in_full = times_left(norm_two_all, grad_fc_pre)
    grad_fc_in_part = jnp.sum(grad_fc_pre.astype(jnp.float32), axis=0)
    grad_norm_two = sum_narrow(times_right(grad_fc_pre, vis_back[4]))
    ignored, pull_two = jax.vjp(layer_norm, after_attn, mlp_norm_gain, mlp_norm_shift)
    grad_mid_norm, grad_mlp_gain, grad_mlp_shift = pull_two(grad_norm_two)
    grad_mid = grad_vis + grad_mid_norm
    grad_out_rows = jnp.sum(grad_mid, axis=0)
    grad_mid_all = gather_narrow(grad_mid.astype(jnp.bfloat16))
    grad_out_full = times_left(attended, grad_mid_all)
    grad_attended = (
        times_right(grad_mid_all, vis_back[3])
        .astype(jnp.bfloat16)
        .reshape(seq_len, vis_heads, 1, HD_V)
    )
    grad_vq, grad_vk, grad_vv = attend_back(
        query_rows, key_rows, value_rows, vis_valid, vis_scale, vis_total, grad_attended
    )
    grad_vq = grad_vq.reshape(seq_len, vis_heads * HD_V)
    grad_vk = grad_vk.reshape(seq_len, vis_heads * HD_V)
    grad_vv = grad_vv.reshape(seq_len, vis_heads * HD_V)
    grad_query_full = times_left(norm_all, grad_vq)
    grad_key_full = times_left(norm_all, grad_vk)
    grad_value_full = times_left(norm_all, grad_vv)
    grad_query_part = jnp.sum(grad_vq.astype(jnp.float32), axis=0)
    grad_value_part = jnp.sum(grad_vv.astype(jnp.float32), axis=0)
    grad_norm_one = sum_narrow(
        times_right(grad_vq, vis_back[0])
        + times_right(grad_vk, vis_back[1])
        + times_right(grad_vv, vis_back[2])
    )
    ignored, pull_one = jax.vjp(layer_norm, patch_rows, attn_norm_gain, attn_norm_shift)
    grad_in_norm, grad_attn_gain, grad_attn_shift = pull_one(grad_norm_one)
    patches_grad = grad_mid + grad_in_norm
    encoder_sums = (
        lax.psum_scatter(grad_query_full, "seq", scatter_dimension=0, tiled=True),
        lax.psum_scatter(grad_key_full, "seq", scatter_dimension=0, tiled=True),
        lax.psum_scatter(grad_value_full, "seq", scatter_dimension=0, tiled=True),
        lax.psum_scatter(grad_out_full, "seq", scatter_dimension=1, tiled=True),
        lax.psum_scatter(grad_fc_in_full, "seq", scatter_dimension=0, tiled=True),
        lax.psum_scatter(grad_fc_out_full, "seq", scatter_dimension=1, tiled=True),
        lax.psum_scatter(grad_pgate_full, "seq", scatter_dimension=0, tiled=True),
        lax.psum_scatter(grad_pup_full, "seq", scatter_dimension=0, tiled=True),
        lax.psum_scatter(grad_pdown_full, "seq", scatter_dimension=0, tiled=True),
    )
    vector_sums = lax.psum(
        (
            grad_attn_gain,
            grad_attn_shift,
            spread_slot(grad_query_part, tensor, tp_index),
            spread_slot(grad_value_part, tensor, tp_index),
            grad_out_rows,
            grad_mlp_gain,
            grad_mlp_shift,
            spread_slot(grad_fc_in_part, tensor, tp_index),
            grad_fc_out_rows,
            grad_context_gain,
            grad_latent_gain,
            grad_post_gain,
        ),
        ("seq", "tp"),
    )
    return (
        latents,
        patches_grad,
        vector_sums[0],
        vector_sums[1],
        encoder_sums[0],
        take_slot(vector_sums[2], tensor, tp_index),
        encoder_sums[1],
        encoder_sums[2],
        take_slot(vector_sums[3], tensor, tp_index),
        encoder_sums[3],
        vector_sums[4],
        vector_sums[5],
        vector_sums[6],
        encoder_sums[4],
        take_slot(vector_sums[7], tensor, tp_index),
        encoder_sums[5],
        vector_sums[8],
        encoder_sums[6],
        encoder_sums[7],
        encoder_sums[8],
        grad_latent_param,
        vector_sums[9],
        vector_sums[10],
        grad_res_query,
        grad_res_key,
        grad_res_value,
        grad_res_out,
        vector_sums[11],
        grad_ffn_gate,
        grad_ffn_up,
        grad_ffn_down,
    )


def solution(mesh):
    return jax.shard_map(
        shards,
        mesh=mesh,
        in_specs=(
            P(("seq", "tp"), None),
            P("seq"),
            P(),
            P(),
            P("seq", "tp"),
            P("tp"),
            P("seq", "tp"),
            P("seq", "tp"),
            P("tp"),
            P("tp", "seq"),
            P(),
            P(),
            P(),
            P("seq", "tp"),
            P("tp"),
            P("tp", "seq"),
            P(),
            P("seq", "tp"),
            P("seq", "tp"),
            P("seq", "tp"),
            P("tp", "seq"),
            P(),
            P(),
            P("seq", "tp"),
            P("seq", "tp"),
            P("seq", "tp"),
            P("tp", "seq"),
            P(),
            P(("seq", "tp"), None),
            P(("seq", "tp"), None),
            P(("seq", "tp"), None),
            P(("seq", "tp"), None),
        ),
        out_specs=(
            P(("seq", "tp"), None),
            P(("seq", "tp"), None),
            P(),
            P(),
            P("seq", "tp"),
            P("tp"),
            P("seq", "tp"),
            P("seq", "tp"),
            P("tp"),
            P("tp", "seq"),
            P(),
            P(),
            P(),
            P("seq", "tp"),
            P("tp"),
            P("tp", "seq"),
            P(),
            P("seq", "tp"),
            P("seq", "tp"),
            P("seq", "tp"),
            P("tp", "seq"),
            P(),
            P(),
            P("seq", "tp"),
            P("seq", "tp"),
            P("seq", "tp"),
            P("tp", "seq"),
            P(),
            P(("seq", "tp"), None),
            P(("seq", "tp"), None),
            P(("seq", "tp"), None),
        ),
        check_vma=False,
    )
```

profile of v0, /device:TPU:0, one launch (start us, length us, event | category | flops | bytes accessed | tf_op | source)
XLA Modules:
  0.0 4230.0 jit_solution(2681761537711673699)
XLA Ops:
  14.2 14.1 all_gather.102
  28.3 10.8 all_gather.103
  49.1 10.6 all_gather.105
  73.2 29.0 reduce-scatter.29.cloned.1.call-done
  107.4 30.2 all-gather.20.cloned.1.call-done
  142.7 25.9 all-gather.24.cloned.1.call-done
  174.5 29.3 reduce-scatter.31.cloned.1.call-done
  207.6 27.4 all-gather.26.cloned.1.call-done
  234.9 54.7 %all-gather.28.cloned.1.call-done = bf16[1152,3584]{1,0:T(8,128)(2,1)} async-done(((bf16[144,3584]{1,0:T(8,128)(2,1)}), bf16[1152,3584]{1,0:T(8,128)(2,1)}) %all-gather.28.cloned.1.call-update) | async-done | bytes 8257552 | tf_op jit(solution)/shard_map/all_gather | solution.py:146
  289.6 11.7 fusion.103
  301.4 43.9 %all-gather.30.cloned.1.call-done = bf16[1152,3584]{1,0:T(8,128)(2,1)} async-done(((bf16[144,3584]{1,0:T(8,128)(2,1)}), bf16[1152,3584]{1,0:T(8,128)(2,1)}) %all-gather.30.cloned.1.call-update) | async-done | bytes 8257552 | tf_op jit(solution)/shard_map/all_gather | solution.py:147
  345.3 13.1 multiply_convert_fusion.1
  358.3 131.9 %all-gather.32.cloned.1.call-done = bf16[4096,3584]{1,0:T(8,128)(2,1)} async-done(((bf16[512,3584]{1,0:T(8,128)(2,1)}), bf16[4096,3584]{1,0:T(8,128)(2,1)}) %all-gather.32.cloned.1.call-update) | async-done | bytes 29360144 | tf_op jit(solution)/shard_map/all_gather | solution.py:148
  490.2 23.6 convolution_convert_fusion
  514.7 76.0 %reduce-scatter.33.cloned.1.call-done = bf16[128,4096]{1,0:T(8,128)(2,1)} async-done(((bf16[512,4096]{1,0:T(8,128)(2,1)}), bf16[128,4096]{1,0:T(8,128)(2,1)}) %reduce-scatter.33.cloned.1.call-update) | async-done | bytes 1048592 | tf_op jit(solution)/shard_map/reduce_scatter | solution.py:129
  605.4 10.4 all_gather.116
  615.8 12.1 all_gather.115
  628.6 18.8 all_gather.114
  650.2 62.8 %all-gather.34.cloned.1.call-done = bf16[512,4096]{1,0:T(8,128)(2,1)} async-done(((bf16[128,4096]{1,0:T(8,128)(2,1)}), bf16[512,4096]{1,0:T(8,128)(2,1)}) %all-gather.34.cloned.1.call-update) | async-done | bytes 4194320 | tf_op jit(solution)/shard_map/all_gather | solution.py:121
  719.9 25.7 all-gather.38.cloned.1.call-done
  751.3 22.2 all_gather.123
  776.9 14.8 all_gather.119
  791.7 145.1 %all-gather.40.cloned.1.call-done = bf16[4096,4096]{1,0:T(8,128)(2,1)} async-done(((bf16[512,4096]{1,0:T(8,128)(2,1)}), bf16[4096,4096]{1,0:T(8,128)(2,1)}) %all-gather.40.cloned.1.call-update) | async-done | bytes 33554448 | tf_op jit(solution)/shard_map/all_gather | solution.py:164
  936.8 18.7 fusion.104
  955.5 144.1 %all-gather.42.cloned.1.call-done = bf16[4096,4096]{1,0:T(8,128)(2,1)} async-done(((bf16[512,4096]{1,0:T(8,128)(2,1)}), bf16[4096,4096]{1,0:T(8,128)(2,1)}) %all-gather.42.cloned.1.call-update) | async-done | bytes 33554448 | tf_op jit(solution)/shard_map/all_gather | solution.py:165
  1099.6 18.7 fusion.105
  1118.3 143.9 %all-gather.44.cloned.1.call-done = bf16[4096,4096]{1,0:T(8,128)(2,1)} async-done(((bf16[512,4096]{1,0:T(8,128)(2,1)}), bf16[4096,4096]{1,0:T(8,128)(2,1)}) %all-gather.44.cloned.1.call-update) | async-done | bytes 33554448 | tf_op jit(solution)/shard_map/all_gather | solution.py:166
  1262.1 16.0 multiply_convert_fusion.3
  1278.1 14.0 fusion.106
  1292.1 14.6 fusion.5
  1306.8 21.7 reduce-scatter.39.cloned.1.call-done
  1332.5 16.0 all_gather.124
  1366.7 75.1 %reduce-scatter.41.cloned.1.call-done = bf16[128,4096]{1,0:T(8,128)(2,1)} async-done(((bf16[512,4096]{1,0:T(8,128)(2,1)}), bf16[128,4096]{1,0:T(8,128)(2,1)}) %reduce-scatter.41.cloned.1.call-update) | async-done | bytes 1048592 | tf_op jit(solution)/shard_map/reduce_scatter | solution.py:129
  1446.3 81.4 %all-gather.46.cloned.1.call-done = bf16[512,4096]{1,0:T(8,128)(2,1)} async-done(((bf16[128,4096]{1,0:T(8,128)(2,1)}), bf16[512,4096]{1,0:T(8,128)(2,1)}) %all-gather.46.cloned.1.call-update) | async-done | bytes 4194320 | tf_op jit(solution)/shard_map/all_gather | solution.py:121
  1527.6 29.5 multiply_convert_fusion
  1576.1 27.8 reduce-scatter.43.cloned.1.call-done
  1604.2 30.3 all-gather.48.cloned.1.call-done
  1646.1 28.4 reduce-scatter.45.cloned.1.call-done
  1686.4 24.1 all-gather.50.cloned.1.call-done
  1724.6 14.6 convolution_convert_fusion.2
  1742.0 22.3 reduce-scatter.47.cloned.1.call-done
  1768.1 19.3 reduce-scatter.37.cloned.1.call-done
  1832.1 10.2 fusion.115
  1842.6 10.2 fusion.116
  1853.9 23.3 fusion.120
  1878.3 23.3 fusion.121
  1902.7 23.3 fusion.122
  1926.2 27.0 fusion.117
  1962.5 42.2 reduce-scatter.73.cloned.1.call-done
  2004.7 42.4 %reduce-scatter.75.cloned.1.call-done = f32[512,96]{0,1:T(8,128)} async-done(((f32[4096,96]{0,1:T(8,128)}), f32[512,96]{0,1:T(8,128)}) %reduce-scatter.75.cloned.1.call-update) | async-done | bytes 196624 | tf_op jit(solution)/shard_map/reduce_scatter | solution.py:344
  2047.1 65.7 %reduce-scatter.71.cloned.1.call-done = f32[512,384]{1,0:T(8,128)} async-done(((f32[4096,384]{1,0:T(8,128)}), f32[512,384]{1,0:T(8,128)}) %reduce-scatter.71.cloned.1.call-update) | async-done | bytes 786448 | tf_op jit(solution)/shard_map/reduce_scatter | solution.py:342
  2112.8 66.1 %reduce-scatter.77.cloned.1.call-done = f32[384,512]{1,0:T(8,128)} async-done(((f32[384,4096]{1,0:T(8,128)}), f32[384,512]{1,0:T(8,128)}) %reduce-scatter.77.cloned.1.call-update) | async-done | bytes 786448 | tf_op jit(solution)/shard_map/reduce_scatter | solution.py:345
  2178.9 43.2 %reduce-scatter.49.cloned.1.call-done = f32[144,288]{1,0:T(8,128)} async-done(((f32[1152,288]{1,0:T(8,128)}), f32[144,288]{1,0:T(8,128)}) %reduce-scatter.49.cloned.1.call-update) | async-done | bytes 165904 | tf_op jit(solution)/shard_map/reduce_scatter | solution.py:400
  2222.1 43.4 %reduce-scatter.51.cloned.1.call-done = f32[144,288]{1,0:T(8,128)} async-done(((f32[1152,288]{1,0:T(8,128)}), f32[144,288]{1,0:T(8,128)}) %reduce-scatter.51.cloned.1.call-update) | async-done | bytes 165904 | tf_op jit(solution)/shard_map/reduce_scatter | solution.py:401
  2265.5 43.2 %reduce-scatter.53.cloned.1.call-done = f32[144,288]{1,0:T(8,128)} async-done(((f32[1152,288]{1,0:T(8,128)}), f32[144,288]{1,0:T(8,128)}) %reduce-scatter.53.cloned.1.call-update) | async-done | bytes 165904 | tf_op jit(solution)/shard_map/reduce_scatter | solution.py:402
  2308.7 43.3 %reduce-scatter.55.cloned.1.call-done = f32[288,144]{0,1:T(8,128)} async-done(((f32[288,1152]{0,1:T(8,128)}), f32[288,144]{0,1:T(8,128)}) %reduce-scatter.55.cloned.1.call-update) | async-done | bytes 165904 | tf_op jit(solution)/shard_map/reduce_scatter | solution.py:403
  2352.0 60.9 %reduce-scatter.57.cloned.1.call-done = f32[144,1076]{1,0:T(8,128)} async-done(((f32[1152,1076]{1,0:T(8,128)}), f32[144,1076]{1,0:T(8,128)}) %reduce-scatter.57.cloned.1.call-update) | async-done | bytes 619792 | tf_op jit(solution)/shard_map/reduce_scatter | solution.py:404
  2412.9 61.3 %reduce-scatter.59.cloned.1.call-done = f32[1076,144]{0,1:T(8,128)} async-done(((f32[1076,1152]{0,1:T(8,128)}), f32[1076,144]{0,1:T(8,128)}) %reduce-scatter.59.cloned.1.call-update) | async-done | bytes 619792 | tf_op jit(solution)/shard_map/reduce_scatter | solution.py:405
  2474.2 118.9 %reduce-scatter.61.cloned.1.call-done = f32[144,3584]{1,0:T(8,128)} async-done(((f32[1152,3584]{1,0:T(8,128)}), f32[144,3584]{1,0:T(8,128)}) %reduce-scatter.61.cloned.1.call-update) | async-done | bytes 2064400 | tf_op jit(solution)/shard_map/reduce_scatter | solution.py:406
  2593.2 119.5 %reduce-scatter.63.cloned.1.call-done = f32[144,3584]{1,0:T(8,128)} async-done(((f32[1152,3584]{1,0:T(8,128)}), f32[144,3584]{1,0:T(8,128)}) %reduce-scatter.63.cloned.1.call-update) | async-done | bytes 2064400 | tf_op jit(solution)/shard_map/reduce_scatter | solution.py:407
  2712.7 387.9 %reduce-scatter.79.cloned.1.call-done = f32[512,4096]{1,0:T(8,128)} async-done(((f32[4096,4096]{1,0:T(8,128)}), f32[512,4096]{1,0:T(8,128)}) %reduce-scatter.79.cloned.1.call-update) | async-done | bytes 8388624 | tf_op jit(solution)/shard_map/reduce_scatter | solution.py:309
  3100.5 388.2 %reduce-scatter.81.cloned.1.call-done = f32[512,4096]{1,0:T(8,128)} async-done(((f32[4096,4096]{1,0:T(8,128)}), f32[512,4096]{1,0:T(8,128)}) %reduce-scatter.81.cloned.1.call-update) | async-done | bytes 8388624 | tf_op jit(solution)/shard_map/reduce_scatter | solution.py:310
  3488.7 387.9 %reduce-scatter.83.cloned.1.call-done = f32[512,4096]{1,0:T(8,128)} async-done(((f32[4096,4096]{1,0:T(8,128)}), f32[512,4096]{1,0:T(8,128)}) %reduce-scatter.83.cloned.1.call-update) | async-done | bytes 8388624 | tf_op jit(solution)/shard_map/reduce_scatter | solution.py:311
  3876.6 334.0 %reduce-scatter.65.cloned.1.call-done = f32[512,3584]{1,0:T(8,128)} async-done(((f32[4096,3584]{1,0:T(8,128)}), f32[512,3584]{1,0:T(8,128)}) %reduce-scatter.65.cloned.1.call-update) | async-done | bytes 7340048 | tf_op jit(solution)/shard_map/reduce_scatter | solution.py:408
  (487 shorter events, 241.4 us)
Async XLA Ops:
  8.1 51.6 %all-gather.18.cloned.1.call-start = ((), (), s32[]{:S(2)}) async-start(), calls=%async_computation.28 | async-start | bytes 1474560 | tf_op jit(solution)/shard_map/all_gather | solution.py:109
  13.5 88.7 %reduce-scatter.29.cloned.1.call-start = ((), (), s32[]{:S(2)}) async-start(), calls=%async_computation.29 | async-start | bytes 1474560 | tf_op jit(solution)/shard_map/reduce_scatter | solution.py:113
  14.2 581.8 %copy-start.88 = (pred[512]{0:T(512)(128)(4,1)}, pred[512]{0:T(512)(128)(4,1)S(1)}, u32[]{:S(2)}) copy-start(pred[512]{0:T(512)(128)(4,1)S(1)} %iota_compare_fusion) | copy-start | bytes 1540
  72.5 65.0 %copy-start.127 = (f32[1076]{0:T(1024)S(1)}, f32[1076]{0:T(1024)}, u32[]{:S(2)}) copy-start(f32[1076]{0:T(1024)} %param.46) | copy-start | bytes 12916
  72.6 34.8 all-gather.22.cloned.1.call-start
  73.1 64.4 %all-gather.20.cloned.1.call-start = ((), (), s32[]{:S(2)}) async-start(), calls=%async_computation.30 | async-start | bytes 1474560 | tf_op jit(solution)/shard_map/all_gather | solution.py:109
  106.5 62.1 %all-gather.24.cloned.1.call-start = ((), (), s32[]{:S(2)}) async-start(), calls=%async_computation.32 | async-start | bytes 2985984 | tf_op jit(solution)/shard_map/all_gather | solution.py:140
  107.1 96.7 %reduce-scatter.31.cloned.1.call-start = ((), (), s32[]{:S(2)}) async-start(), calls=%async_computation.33 | async-start | bytes 1474560 | tf_op jit(solution)/shard_map/reduce_scatter | solution.py:113
  174.4 60.5 %all-gather.26.cloned.1.call-start = ((), (), s32[]{:S(2)}) async-start(), calls=%async_computation.34 | async-start | bytes 1474560 | tf_op jit(solution)/shard_map/all_gather | solution.py:109
  205.6 84.1 %all-gather.28.cloned.1.call-start = ((), (), s32[]{:S(2)}) async-start(), calls=%async_computation.35 | async-start | bytes 9289728 | tf_op jit(solution)/shard_map/all_gather | solution.py:146
  206.2 139.1 %all-gather.30.cloned.1.call-start = ((), (), s32[]{:S(2)}) async-start(), calls=%async_computation.36 | async-start | bytes 9289728 | tf_op jit(solution)/shard_map/all_gather | solution.py:147
  206.8 283.5 %all-gather.32.cloned.1.call-start = ((), (), s32[]{:S(2)}) async-start(), calls=%async_computation.37 | async-start | bytes 33030144 | tf_op jit(solution)/shard_map/all_gather | solution.py:148
  207.5 383.3 %reduce-scatter.33.cloned.1.call-start = ((), (), s32[]{:S(2)}) async-start(), calls=%async_computation.38 | async-start | bytes 5242880 | tf_op jit(solution)/shard_map/reduce_scatter | solution.py:129
  234.9 110.3 %copy-start.124 = (bf16[512,1152]{1,0:T(8,128)(2,1)S(1)}, bf16[512,1152]{1,0:T(8,128)(2,1)}, u32[]{:S(2)}) copy-start(bf16[512,1152]{1,0:T(8,128)(2,1)} %all-gather.26.cloned.1.call-done) | copy-start | bytes 3538948
  513.9 79.0 %copy-start.70 = (f32[4096]{0:T(1024)S(1)}, f32[4096]{0:T(1024)}, u32[]{:S(2)}) copy-start(f32[4096]{0:T(1024)} %param.53) | copy-start | bytes 49156
  513.9 82.2 %copy-start.90 = (bf16[16,512]{1,0:T(8,128)(2,1)S(1)}, bf16[16,512]{1,0:T(8,128)(2,1)}, u32[]{:S(2)}) copy-start(bf16[16,512]{1,0:T(8,128)(2,1)} %param.52) | copy-start | bytes 49156
  513.9 91.5 %copy-start.82 = (bf16[512,96]{0,1:T(8,128)(2,1)S(1)}, bf16[512,96]{0,1:T(8,128)(2,1)}, u32[]{:S(2)}) copy-start(bf16[512,96]{0,1:T(8,128)(2,1)} %param.56) | copy-start | bytes 294916
  513.9 133.5 %all-gather.36.cloned.1.call-start = ((), (), s32[]{:S(2)}) async-start(), calls=%async_computation.40 | async-start | bytes 3538944 | tf_op jit(solution)/shard_map/all_gather | solution.py:155
  514.7 101.2 %copy-start.83 = (bf16[512,96]{0,1:T(8,128)(2,1)S(1)}, bf16[512,96]{0,1:T(8,128)(2,1)}, u32[]{:S(2)}) copy-start(bf16[512,96]{0,1:T(8,128)(2,1)} %param.57) | copy-start | bytes 294916
  514.7 198.3 %all-gather.34.cloned.1.call-start = ((), (), s32[]{:S(2)}) async-start(), calls=%async_computation.39 | async-start | bytes 5242880 | tf_op jit(solution)/shard_map/all_gather | solution.py:121
  595.4 150.3 %all-gather.38.cloned.1.call-start = ((), (), s32[]{:S(2)}) async-start(), calls=%async_computation.41 | async-start | bytes 3538944 | tf_op jit(solution)/shard_map/all_gather | solution.py:158
  596.0 177.8 %reduce-scatter.35.cloned.1.call-start = ((), (), s32[]{:S(2)}) async-start(), calls=%async_computation.42 | async-start | bytes 655360 | tf_op jit(solution)/shard_map/reduce_scatter | solution.py:129
  647.4 68.0 %copy-start.16 = (bf16[64,4096]{1,0:T(8,128)(2,1)}, bf16[64,4096]{1,0:T(8,128)(2,1)S(1)}, u32[]{:S(2)}) copy-start(bf16[64,4096]{1,0:T(8,128)(2,1)S(1)} %all_gather.114) | copy-start | bytes 1572868
  650.2 66.9 %copy-start.63 = (bf16[64,4,96]{2,1,0:T(4,128)(2,1)}, bf16[64,4,96]{2,1,0:T(4,128)(2,1)S(1)}, u32[]{:S(2)}) copy-start(bf16[64,4,96]{2,1,0:T(4,128)(2,1)S(1)} %reshape.369) | copy-start | bytes 147460
  749.1 187.8 %all-gather.40.cloned.1.call-start = ((), (), s32[]{:S(2)}) async-start(), calls=%async_computation.43 | async-start | bytes 37748736 | tf_op jit(solution)/shard_map/all_gather | solution.py:164
  749.7 349.9 %all-gather.42.cloned.1.call-start = ((), (), s32[]{:S(2)}) async-start(), calls=%async_computation.44 | async-start | bytes 37748736 | tf_op jit(solution)/shard_map/all_gather | solution.py:165
  750.4 511.7 %all-gather.44.cloned.1.call-start = ((), (), s32[]{:S(2)}) async-start(), calls=%async_computation.45 | async-start | bytes 37748736 | tf_op jit(solution)/shard_map/all_gather | solution.py:166
  751.0 577.6 %reduce-scatter.39.cloned.1.call-start = ((), (), s32[]{:S(2)}) async-start(), calls=%async_computation.47 | async-start | bytes 655360 | tf_op jit(solution)/shard_map/reduce_scatter | solution.py:129
  791.7 307.9 %copy-start.14 = (bf16[64,4096]{1,0:T(8,128)(2,1)}, bf16[64,4096]{1,0:T(8,128)(2,1)S(1)}, u32[]{:S(2)}) copy-start(bf16[64,4096]{1,0:T(8,128)(2,1)S(1)} %all_gather.119) | copy-start | bytes 1572868
  1306.8 135.1 %reduce-scatter.41.cloned.1.call-start = ((), (), s32[]{:S(2)}) async-start(), calls=%async_computation.48 | async-start | bytes 5242880 | tf_op jit(solution)/shard_map/reduce_scatter | solution.py:129
  1366.7 75.2 %copy-start.11 = (bf16[128,4096]{1,0:T(8,128)(2,1)S(1)}, bf16[128,4096]{1,0:T(8,128)(2,1)}, u32[]{:S(2)}) copy-start(bf16[128,4096]{1,0:T(8,128)(2,1)} %reduce-scatter.33.cloned.1.call-done) | copy-start | bytes 3145732
  1366.7 75.2 %copy-start.71 = (f32[4096]{0:T(1024)S(1)}, f32[4096]{0:T(1024)}, u32[]{:S(2)}) copy-start(f32[4096]{0:T(1024)} %param.53) | copy-start | bytes 49156
  1366.7 75.2 %copy-start.108 = (f32[128]{0:T(128)S(1)}, f32[128]{0:T(128)}, u32[]{:S(2)}) copy-start(f32[128]{0:T(128)} %copy-done.107) | copy-start | bytes 1540
  1366.7 78.0 %copy-start.121 = (f32[128]{0:T(128)S(1)}, f32[128]{0:T(128)}, u32[]{:S(2)}) copy-start(f32[128]{0:T(128)} %copy-done.120) | copy-start | bytes 1540
  1366.7 160.9 %all-gather.46.cloned.1.call-start = ((), (), s32[]{:S(2)}) async-start(), calls=%async_computation.49 | async-start | bytes 5242880 | tf_op jit(solution)/shard_map/all_gather | solution.py:121
  1446.2 157.7 %reduce-scatter.43.cloned.1.call-start = ((), (), s32[]{:S(2)}) async-start(), calls=%async_computation.50 | async-start | bytes 1474560 | tf_op jit(solution)/shard_map/reduce_scatter | solution.py:113
  1576.0 58.5 %all-gather.48.cloned.1.call-start = ((), (), s32[]{:S(2)}) async-start(), calls=%async_computation.51 | async-start | bytes 1474560 | tf_op jit(solution)/shard_map/all_gather | solution.py:109
  1603.9 70.6 %reduce-scatter.45.cloned.1.call-start = ((), (), s32[]{:S(2)}) async-start(), calls=%async_computation.52 | async-start | bytes 1474560 | tf_op jit(solution)/shard_map/reduce_scatter | solution.py:113
  1646.1 64.4 %all-gather.50.cloned.1.call-start = ((), (), s32[]{:S(2)}) async-start(), calls=%async_computation.53 | async-start | bytes 1474560 | tf_op jit(solution)/shard_map/all_gather | solution.py:109
  1681.2 58.1 %reduce-scatter.67.cloned.1.call-start = ((), (), s32[]{:S(2)}) async-start(), calls=%async_computation.64 | async-start | bytes 655360 | tf_op jit(solution)/shard_map/reduce_scatter | solution.py:129
  1685.9 78.4 %reduce-scatter.47.cloned.1.call-start = ((), (), s32[]{:S(2)}) async-start(), calls=%async_computation.54 | async-start | bytes 1474560 | tf_op jit(solution)/shard_map/reduce_scatter | solution.py:113
  1724.4 63.1 %reduce-scatter.37.cloned.1.call-start = ((), (), s32[]{:S(2)}) async-start(), calls=%async_computation.46 | async-start | bytes 655360 | tf_op jit(solution)/shard_map/reduce_scatter | solution.py:129
  1724.5 62.9 %copy-start.57 = (bf16[16,4096]{1,0:T(8,128)(2,1)S(1)}, bf16[16,4096]{1,0:T(8,128)(2,1)}, u32[]{:S(2)}) copy-start(bf16[16,4096]{1,0:T(8,128)(2,1)} %param.63) | copy-start | bytes 393220
  1724.5 62.9 %copy-start.58 = (bf16[16,4096]{1,0:T(8,128)(2,1)S(1)}, bf16[16,4096]{1,0:T(8,128)(2,1)}, u32[]{:S(2)}) copy-start(bf16[16,4096]{1,0:T(8,128)(2,1)} %reduce-scatter.39.cloned.1.call-done) | copy-start | bytes 393220
  1724.5 62.9 %copy-start.99 = (f32[16]{0:T(128)S(1)}, f32[16]{0:T(128)}, u32[]{:S(2)}) copy-start(f32[16]{0:T(128)} %copy-done.98) | copy-start | bytes 196
  1724.5 62.9 %copy-start.110 = (f32[16]{0:T(128)S(1)}, f32[16]{0:T(128)}, u32[]{:S(2)}) copy-start(f32[16]{0:T(128)} %copy-done.109) | copy-start | bytes 196
  1739.2 216.4 %all-reduce.4.cloned.1.call-start = ((), (), s32[]{:S(2)}) async-start(), calls=%async_computation.73 | async-start | bytes 270336 | tf_op jit(solution)/shard_map/psum | solution.py:410
  1768.1 194.4 %reduce-scatter.69.cloned.1.call-start = ((), (), s32[]{:S(2)}) async-start(), calls=%async_computation.65 | async-start | bytes 294912 | tf_op jit(solution)/shard_map/reduce_scatter | solution.py:341
  1789.4 215.3 %reduce-scatter.73.cloned.1.call-start = ((), (), s32[]{:S(2)}) async-start(), calls=%async_computation.67 | async-start | bytes 1769472 | tf_op jit(solution)/shard_map/reduce_scatter | solution.py:343
  1794.2 252.9 %reduce-scatter.75.cloned.1.call-start = ((), (), s32[]{:S(2)}) async-start(), calls=%async_computation.68 | async-start | bytes 1769472 | tf_op jit(solution)/shard_map/reduce_scatter | solution.py:344
  1798.9 313.9 %reduce-scatter.71.cloned.1.call-start = ((), (), s32[]{:S(2)}) async-start(), calls=%async_computation.66 | async-start | bytes 7077888 | tf_op jit(solution)/shard_map/reduce_scatter | solution.py:342
  1802.7 376.3 %reduce-scatter.77.cloned.1.call-start = ((), (), s32[]{:S(2)}) async-start(), calls=%async_computation.69 | async-start | bytes 7077888 | tf_op jit(solution)/shard_map/reduce_scatter | solution.py:345
  1807.4 414.7 %reduce-scatter.49.cloned.1.call-start = ((), (), s32[]{:S(2)}) async-start(), calls=%async_computation.55 | async-start | bytes 1990656 | tf_op jit(solution)/shard_map/reduce_scatter | solution.py:400
  1810.8 454.7 %reduce-scatter.51.cloned.1.call-start = ((), (), s32[]{:S(2)}) async-start(), calls=%async_computation.56 | async-start | bytes 1990656 | tf_op jit(solution)/shard_map/reduce_scatter | solution.py:401
  1813.0 495.7 %reduce-scatter.53.cloned.1.call-start = ((), (), s32[]{:S(2)}) async-start(), calls=%async_computation.57 | async-start | bytes 1990656 | tf_op jit(solution)/shard_map/reduce_scatter | solution.py:402
  1815.1 536.9 %reduce-scatter.55.cloned.1.call-start = ((), (), s32[]{:S(2)}) async-start(), calls=%async_computation.58 | async-start | bytes 1990656 | tf_op jit(solution)/shard_map/reduce_scatter | solution.py:403
  1818.3 594.6 %reduce-scatter.57.cloned.1.call-start = ((), (), s32[]{:S(2)}) async-start(), calls=%async_computation.59 | async-start | bytes 5971968 | tf_op jit(solution)/shard_map/reduce_scatter | solution.py:404
  1823.7 650.5 %reduce-scatter.59.cloned.1.call-start = ((), (), s32[]{:S(2)}) async-start(), calls=%async_computation.60 | async-start | bytes 5971968 | tf_op jit(solution)/shard_map/reduce_scatter | solution.py:405
  1830.8 762.3 %reduce-scatter.61.cloned.1.call-start = ((), (), s32[]{:S(2)}) async-start(), calls=%async_computation.61 | async-start | bytes 18579456 | tf_op jit(solution)/shard_map/reduce_scatter | solution.py:406
  1842.3 870.4 %reduce-scatter.63.cloned.1.call-start = ((), (), s32[]{:S(2)}) async-start(), calls=%async_computation.62 | async-start | bytes 18579456 | tf_op jit(solution)/shard_map/reduce_scatter | solution.py:407
  1852.8 1247.8 %reduce-scatter.79.cloned.1.call-start = ((), (), s32[]{:S(2)}) async-start(), calls=%async_computation.70 | async-start | bytes 75497472 | tf_op jit(solution)/shard_map/reduce_scatter | solution.py:309
  1877.3 1611.5 %reduce-scatter.81.cloned.1.call-start = ((), (), s32[]{:S(2)}) async-start(), calls=%async_computation.71 | async-start | bytes 75497472 | tf_op jit(solution)/shard_map/reduce_scatter | solution.py:310
  1901.6 1975.0 %reduce-scatter.83.cloned.1.call-start = ((), (), s32[]{:S(2)}) async-start(), calls=%async_computation.72 | async-start | bytes 75497472 | tf_op jit(solution)/shard_map/reduce_scatter | solution.py:311
  1925.9 2284.7 %reduce-scatter.65.cloned.1.call-start = ((), (), s32[]{:S(2)}) async-start(), calls=%async_computation.63 | async-start | bytes 66060288 | tf_op jit(solution)/shard_map/reduce_scatter | solution.py:408
  (114 other events, 1698.3 us)
Sparse Core Ops, SparseCore 0:
  13.6 33.1 all-gather.17
  72.7 29.5 reduce-scatter.28
  174.5 29.1 reduce-scatter.30
  205.7 29.1 all-gather.25
  236.7 52.9 all-gather.27
  291.4 53.8 all-gather.29
  347.1 143.0 all-gather.31
  1306.9 21.6 reduce-scatter.38
  1366.8 74.9 reduce-scatter.40
  1446.3 81.2 all-gather.45
  1576.1 27.7 reduce-scatter.42
  1605.3 29.1 all-gather.47
  1646.2 28.2 reduce-scatter.44
  1681.3 29.1 all-gather.49
  1713.2 20.7 reduce-scatter.66
  1736.7 27.5 reduce-scatter.46
  1767.0 20.4 reduce-scatter.36
  1796.0 126.1 all-reduce.3
  1926.1 36.3 reduce-scatter.68
  1966.2 38.4 reduce-scatter.72
  2008.6 38.4 reduce-scatter.74
  2051.1 61.6 reduce-scatter.70
  2117.1 61.7 reduce-scatter.76
  2182.7 39.3 reduce-scatter.48
  2226.1 39.3 reduce-scatter.50
  2269.3 39.3 reduce-scatter.52
  2312.5 39.4 reduce-scatter.54
  2356.0 56.9 reduce-scatter.56
  2417.3 56.8 reduce-scatter.58
  2478.4 114.6 reduce-scatter.60
  2598.0 114.6 reduce-scatter.62
  2716.8 383.6 reduce-scatter.78
  3105.0 383.7 reduce-scatter.80
  3492.9 383.6 reduce-scatter.82
  3881.3 329.3 reduce-scatter.64
Sparse Core Ops, SparseCore 1:
  74.9 30.4 all-gather.21
  107.4 30.2 all-gather.19
  139.3 29.3 all-gather.23
  514.0 76.7 reduce-scatter.32
  592.8 35.1 all-gather.35
  630.3 82.7 all-gather.33
  714.9 30.7 all-gather.37
  749.1 24.6 reduce-scatter.34
  775.7 161.1 all-gather.39
  938.9 160.6 all-gather.41
  1101.5 160.6 all-gather.43
where the time goes:
time: 4240 us; the launch traced here: 4230 us
  waiting for transfers between devices  3560 us (84%)
  matrix products  412 us (10%)
  blocking collectives  149 us (4%)
  local copies, waits for them, and re-layouts  44.9 us (1%)
  other arithmetic  43.8 us (1%)
    reduce_scatter x1, waiting for transfers between devices, shards(): lax.psum_scatter(grad_up_full, 'seq', scatter_dimension=0, tiled=True)  388 us
    reduce_scatter x1, waiting for transfers between devices, shards(): lax.psum_scatter(grad_down_full, 'seq', scatter_dimension=0, tiled=True)  388 us
    reduce_scatter x1, waiting for transfers between devices, shards(): lax.psum_scatter(grad_gate_full, 'seq', scatter_dimension=0, tiled=True)  388 us
    reduce_scatter x1, waiting for transfers between devices, shards(): lax.psum_scatter(grad_pdown_full, 'seq', scatter_dimension=0, tiled=True)  334 us
    reduce_scatter x6, waiting for transfers between devices, sum_wide(): lax.psum_scatter(as_sent(terms), 'tp', scatter_dimension=0, tiled=True)  192 us
    dot_general x16, matrix products, times_left(): lax.dot_general(left_side, right_side, (((0,), (0,)), ((), ())), preferre...  154 us
    all_gather x1, waiting for transfers between devices, fetch_ffn(): lax.all_gather(ffn_gate, 'seq', axis=0, tiled=True)  145 us
    all_gather x2, waiting for transfers between devices, gather_wide(): lax.all_gather(as_sent(rows_in), 'tp', axis=0, tiled=True)  144 us
  transfers between devices with their start and end apart: 46, of which 41 were waited for; matrix products, arithmetic and copies ran while one was open for 7% of the time, Pallas kernels for 0%

commit v1 on v0

v1 whole, which is shorter than its diff:
```python
import functools

import jax
import jax.numpy as jnp
from jax import lax
from jax.experimental import pallas as pl
from jax.experimental.pallas import tpu as pltpu
from jax.sharding import PartitionSpec as P

HD_V = 72
H_R = 16
KV_R = 4
HD_R = 96


eps_norm = 1e-06
masked_out = -1e30


def as_sent(value):
    return jax.tree.map(lambda a: a.astype(jnp.bfloat16) if a.dtype == jnp.float32 else a, value)


def layer_norm(inputs, norm_gain, norm_shift):
    row_mean = jnp.mean(inputs, axis=-1, keepdims=True)
    centered = inputs - row_mean
    row_var = jnp.mean(centered * centered, axis=-1, keepdims=True)
    return centered * lax.rsqrt(row_var + eps_norm) * norm_gain + norm_shift


def rms_norm(inputs, norm_gain):
    return (
        inputs * lax.rsqrt(jnp.mean(inputs * inputs, axis=-1, keepdims=True) + eps_norm) * norm_gain
    )


def gelu_tanh(inputs):
    return jax.nn.gelu(inputs, approximate=True)


def swish_gate(gate_pre, up_pre):
    return jax.nn.silu(gate_pre) * up_pre


def swish_back(gate_pre, up_pre, grad_hidden):
    ignored, pull_back = jax.vjp(swish_gate, gate_pre, up_pre)
    grad_gate, grad_up = pull_back(grad_hidden)
    return (grad_gate.astype(jnp.bfloat16), grad_up.astype(jnp.bfloat16))


def times_plain(left_side, right_side):
    return jnp.dot(left_side, right_side, preferred_element_type=jnp.float32)


def times_left(left_side, right_side):
    return lax.dot_general(
        left_side, right_side, (((0,), (0,)), ((), ())), preferred_element_type=jnp.float32
    )


def times_right(left_side, right_side):
    return lax.dot_general(
        left_side, right_side, (((1,), (1,)), ((), ())), preferred_element_type=jnp.float32
    )


def attend(query_rows, key_rows, value_rows, valid_keys, score_scale):
    scores = (
        jnp.einsum("qcge,kce->cgqk", query_rows, key_rows, preferred_element_type=jnp.float32)
        * score_scale
    )
    scores = jnp.where(valid_keys, scores, masked_out)
    top_score = jnp.max(scores, axis=-1, keepdims=True)
    total = jnp.sum(jnp.exp(scores - top_score), axis=-1, keepdims=True)
    log_total = top_score + jnp.log(total)
    weights = jnp.exp(scores - log_total).astype(jnp.bfloat16)
    mixed_rows = jnp.einsum(
        "cgqk,kce->qcge", weights, value_rows, preferred_element_type=jnp.float32
    )
    return (mixed_rows.astype(jnp.bfloat16), log_total)


def attend_back(query_rows, key_rows, value_rows, valid_keys, score_scale, log_total, grad_mixed):
    scores = (
        jnp.einsum("qcge,kce->cgqk", query_rows, key_rows, preferred_element_type=jnp.float32)
        * score_scale
    )
    scores = jnp.where(valid_keys, scores, masked_out)
    probs_full = jnp.exp(scores - log_total)
    grad_probs = jnp.einsum(
        "qcge,kce->cgqk", grad_mixed, value_rows, preferred_element_type=jnp.float32
    )
    inner_sum = jnp.sum(probs_full * grad_probs, axis=-1, keepdims=True)
    grad_scores = (probs_full * (grad_probs - inner_sum)).astype(jnp.bfloat16)
    grad_query = (
        jnp.einsum("cgqk,kce->qcge", grad_scores, key_rows, preferred_element_type=jnp.float32)
        * score_scale
    ).astype(jnp.bfloat16)
    grad_key = (
        jnp.einsum("cgqk,qcge->kce", grad_scores, query_rows, preferred_element_type=jnp.float32)
        * score_scale
    ).astype(jnp.bfloat16)
    grad_value = jnp.einsum(
        "cgqk,qcge->kce",
        probs_full.astype(jnp.bfloat16),
        grad_mixed,
        preferred_element_type=jnp.float32,
    ).astype(jnp.bfloat16)
    return (grad_query, grad_key, grad_value)


def bits_of(count):
    return [1 << i for i in range(count.bit_length() - 1)]


def swap(value, bit, axis, count):
    return lax.ppermute(value, axis, [(i, i ^ bit) for i in range(count)])


def tie(*values):
    return lax.optimization_barrier(values)


def tp_gather(rows_in, count):
    held = {0: rows_in}
    for bit in bits_of(count)[::-1]:
        for j in sorted(held):
            held[j ^ bit] = swap(held[j], bit, "tp", count)
    return [held[j] for j in range(count)]


def tp_scatter(part_of, count):
    parts = {}
    for j in range(count - 1, -1, -1):
        parts[j] = part_of(j)
    for bit in bits_of(count):
        for j in sorted(parts, reverse=True):
            if j & bit:
                parts[j ^ bit] = parts[j ^ bit].astype(jnp.float32) + swap(
                    parts.pop(j).astype(jnp.bfloat16), bit, "tp", count
                ).astype(jnp.float32)
    return parts[0]


def tp_direct(parts, count):
    return [parts[0]] + [swap(parts[j], j, "tp", count) for j in range(1, count)]


def tp_direct_sum(parts, count):
    total = parts[0].astype(jnp.float32)
    for got in tp_direct([parts[0]] + [p.astype(jnp.bfloat16) for p in parts[1:]], count)[1:]:
        total = total + got.astype(jnp.float32)
    return total


def split_orders(count):
    bits = bits_of(count)
    return bits[1:] + bits[:1], bits[:0:-1] + bits[:1]


def swap_each(block_of, count):
    return [block_of(0)] + [swap(block_of(k), k, "seq", count) for k in range(1, count)]


def gather_seq(block, axis=0):
    return lax.all_gather(block, "seq", axis=axis, tiled=True)


def scatter_seq(terms, axis=0):
    return lax.psum_scatter(terms.astype(jnp.bfloat16), "seq", scatter_dimension=axis, tiled=True)


def sum_seq(value, count):
    for bit in bits_of(count):
        value = value + swap(value, bit, "seq", count)
    return value


def add_products(places, rows, *refs):
    lefts, rights, total = refs[: -len(places) - 1], refs[-len(places) - 1 : -1], None
    for (place, part), right in zip(places, rights):
        left = lefts[place][:, part * rows : (part + 1) * rows]
        term = jnp.dot(left, right[...], preferred_element_type=jnp.float32)
        total = term if total is None else total + term
    refs[-1][...] = total


def sum_of_products(lefts, rights, places, tile=512):
    height, rows, width = lefts[0].shape[0], rights[0].shape[0], rights[0].shape[1]
    return pl.pallas_call(
        functools.partial(add_products, places, rows),
        grid=(width // tile,),
        in_specs=[pl.BlockSpec(left.shape, lambda n: (0, 0)) for left in lefts]
        + [pl.BlockSpec((rows, tile), lambda n: (0, n)) for right in rights],
        out_specs=pl.BlockSpec((height, tile), lambda n: (0, n)),
        out_shape=jax.ShapeDtypeStruct((height, width), jnp.float32),
        compiler_params=pltpu.CompilerParams(vmem_limit_bytes=48 * 1024 * 1024),
        cost_estimate=pl.CostEstimate(
            flops=2 * height * rows * width * len(rights),
            bytes_accessed=2 * rows * width * len(rights) + 4 * height * width,
            transcendentals=0,
        ),
    )(*lefts, *rights)


def sum_every(vector, tensor):
    size = vector.shape[0]
    table = jnp.pad(vector, (0, -size % 1024)).reshape(-1, 128)
    for bit in bits_of(tensor):
        table = table + swap(table, bit, "tp", tensor)
    every = lax.all_gather(table, "seq", axis=0, tiled=True)
    return jnp.sum(every.reshape((-1,) + table.shape), axis=0).reshape(-1)[:size]


def pad_cols(value, unit=128):
    spare = -value.shape[1] % unit
    return jnp.pad(value, ((0, 0), (0, spare))) if spare else value


def spread_slot(vector, tensor, tp_index):
    whole_vec = jnp.zeros((vector.shape[0] * tensor,), jnp.float32)
    return lax.dynamic_update_slice_in_dim(whole_vec, vector, tp_index * vector.shape[0], 0)


def take_slot(vector, tensor, tp_index):
    slot_width = vector.shape[0] // tensor
    return lax.dynamic_slice_in_dim(vector, tp_index * slot_width, slot_width, 0)


def shards(
    patches,
    image_patches,
    attn_norm_gain,
    attn_norm_shift,
    query_weight,
    query_bias,
    key_weight,
    value_weight,
    value_bias,
    out_weight,
    out_bias,
    mlp_norm_gain,
    mlp_norm_shift,
    fc_in_weight,
    fc_in_bias,
    fc_out_weight,
    fc_out_bias,
    proj_gate,
    proj_up,
    proj_down,
    latent_param,
    context_gain,
    latent_gain,
    res_query,
    res_key,
    res_value,
    res_out,
    post_gain,
    ffn_gate,
    ffn_up,
    ffn_down,
    cotangent,
):
    tensor = lax.axis_size("tp")
    count = lax.axis_size("seq")
    tp_index = lax.axis_index("tp")
    seq_index = lax.axis_index("seq")
    bf16, f32 = jnp.bfloat16, jnp.float32
    own_rows = patches.shape[0]
    seq_len = own_rows * tensor
    chunks = range(tensor)
    row_ids = jnp.concatenate([(tp_index ^ j) * own_rows + jnp.arange(own_rows) for j in chunks])
    row_valid = row_ids < image_patches[0]
    vis_valid = row_valid[None, None, None, :]
    vis_heads = query_weight.shape[1] // HD_V
    head_width = vis_heads * HD_V
    fc_width = fc_in_weight.shape[1]
    group_size = H_R // KV_R
    vis_scale = HD_V ** (-0.5)
    res_scale = HD_R ** (-0.5)
    d_vis = patches.shape[1]
    d_text = cotangent.shape[1]
    own_cols = latent_param.shape[1]

    def rows_of(value, j):
        return value[j * own_rows : (j + 1) * own_rows]

    proj_width = proj_gate.shape[1]
    owned = [
        proj_gate,
        proj_up,
        pad_cols(jnp.concatenate([query_weight, key_weight, value_weight], axis=1)),
        pad_cols(out_weight.T),
        pad_cols(fc_in_weight),
        pad_cols(fc_out_weight.T),
    ]
    narrow_full = gather_seq(jnp.concatenate(owned, axis=1))
    pdown_full = gather_seq(proj_down)
    starts = [0]
    for block in owned:
        starts.append(starts[-1] + block.shape[1])
    lat_rows = lax.all_gather(latent_param, "seq", axis=1, tiled=True).astype(f32)
    lat_r = lax.rsqrt(jnp.mean(lat_rows * lat_rows, axis=-1, keepdims=True) + eps_norm)
    latent_gain_own = lax.dynamic_slice_in_dim(latent_gain, seq_index * own_cols, own_cols, 0)
    lat_own = latent_param.astype(f32)
    lat_norm_own = (lat_own * lat_r * latent_gain_own).astype(bf16)
    lat_norm_own = jnp.concatenate(tp_direct([lat_norm_own] * tensor, tensor), axis=0)
    latent_rows = latent_param.shape[0]
    latent_count = lat_norm_own.shape[0]
    rkv_own = jnp.concatenate([res_key, res_value], axis=1)
    rkv_width = rkv_own.shape[1]
    res_own = jnp.concatenate([res_query, rkv_own], axis=1)
    query_width = res_query.shape[1]
    lat_proj_sum = sum_seq(times_plain(lat_norm_own, res_own), count)
    rkv_heads = jnp.concatenate(tp_direct([rkv_own] * tensor, tensor), axis=1)
    cot_rows = jnp.concatenate(tp_direct([cotangent] * tensor, tensor), axis=0)
    narrow_full, lat_proj_sum, rkv_heads, cot_rows = tie(
        narrow_full, lat_proj_sum, rkv_heads, cot_rows
    )
    lat_proj = lat_proj_sum.astype(bf16)

    pair_full = narrow_full[:, : 2 * proj_width]
    qkv_full = narrow_full[:, starts[2] : starts[2] + 3 * head_width]
    out_full = narrow_full[:, starts[3] : starts[3] + head_width]
    fc_in_full = narrow_full[:, starts[4] : starts[4] + fc_width]
    fc_out_full = narrow_full[:, starts[5] : starts[5] + fc_width]

    patch_rows = patches.astype(f32)

    norm_one = layer_norm(patch_rows, attn_norm_gain, attn_norm_shift).astype(bf16)
    norm_all = jnp.concatenate(tp_gather(norm_one, tensor), axis=0)
    qkv_bias = jnp.concatenate([query_bias, jnp.zeros_like(query_bias), value_bias])
    qkv_rows = (times_plain(norm_all, qkv_full) + qkv_bias).astype(bf16)
    query_rows = qkv_rows[:, :head_width].reshape(seq_len, vis_heads, 1, HD_V)
    key_rows = qkv_rows[:, head_width : 2 * head_width].reshape(seq_len, vis_heads, HD_V)
    value_rows = qkv_rows[:, 2 * head_width :].reshape(seq_len, vis_heads, HD_V)
    attended, vis_total = attend(query_rows, key_rows, value_rows, vis_valid, vis_scale)
    attended = attended.reshape(seq_len, head_width)
    attn_sum = tp_scatter(lambda j: times_right(rows_of(attended, j), out_full), tensor)
    after_attn = patch_rows + attn_sum + out_bias
    norm_two = tp_gather(layer_norm(after_attn, mlp_norm_gain, mlp_norm_shift).astype(bf16), tensor)
    fc_pre = [times_plain(norm_two[j], fc_in_full) + fc_in_bias for j in chunks]
    fc_act = [gelu_tanh(fc_pre[j]).astype(bf16) for j in chunks]
    fc_sum = tp_direct_sum([times_right(fc_act[j], fc_out_full) for j in chunks], tensor)
    vis_out = after_attn + fc_sum + fc_out_bias
    vis_rows = tp_gather(vis_out.astype(bf16), tensor)

    vis_all = jnp.concatenate(vis_rows, axis=0)
    pair_pre = times_plain(vis_all, pair_full)
    gate_pre, up_pre = pair_pre[:, :proj_width], pair_pre[:, proj_width:]
    hidden_all = swish_gate(gate_pre, up_pre).astype(bf16)

    hidden_all, rkv_heads, ro_late, cot_rows = tie(hidden_all, rkv_heads, res_out, cot_rows)
    rkv_full = gather_seq(rkv_heads)
    ro_full = gather_seq(ro_late, 1)
    cot_every = gather_seq(cot_rows)

    group = d_text // 4
    context = []
    for g in range(4):
        terms = times_right(hidden_all, pdown_full[g * group : (g + 1) * group]).astype(bf16)
        context.append(tp_scatter(lambda j: rows_of(terms, j), tensor))
    context = jnp.concatenate(context, axis=1)

    ctx_norm = rms_norm(context, context_gain).astype(bf16)
    kv_own = times_plain(ctx_norm, rkv_full).astype(bf16)
    kv_image = jnp.concatenate(
        tp_direct([kv_own[:, j * rkv_width : (j + 1) * rkv_width] for j in chunks], tensor), axis=0
    )
    kv_rows = jnp.concatenate([kv_image, lat_proj[:, query_width:]], axis=0)
    res_valid = jnp.concatenate([row_valid, jnp.ones((latent_count,), jnp.bool_)])[
        None, None, None, :
    ]
    kv_local = res_key.shape[1] // HD_R
    res_queries = lat_proj[:, :query_width].reshape(latent_count, kv_local, group_size, HD_R)
    res_keys = kv_rows[:, : kv_local * HD_R].reshape(-1, kv_local, HD_R)
    res_values = kv_rows[:, kv_local * HD_R :].reshape(-1, kv_local, HD_R)
    res_mixed, res_total = attend(res_queries, res_keys, res_values, res_valid, res_scale)
    res_mixed = res_mixed.reshape(latent_count, query_width)
    mixed_out = times_plain(res_mixed, ro_full)
    lat_after = lat_rows + tp_direct_sum(
        [mixed_out[j * latent_rows : (j + 1) * latent_rows] for j in chunks], tensor
    )
    post_norm = rms_norm(lat_after, post_gain).astype(bf16)

    post_norm, cot_every = tie(post_norm, cot_every)
    ffn_input = gather_seq(jnp.concatenate(tp_direct([post_norm] * tensor, tensor), axis=0))
    grad_fhidden = times_right(cot_every, ffn_down)
    half = seq_len // 2
    hidden_held = [hidden_all[:half], hidden_all[half:]]
    if count == 8:
        low_bits, high_bits = split_orders(count)
        ffn_input, *hidden_held = tie(ffn_input, *hidden_held)
        ways = (low_bits, high_bits)
        hidden_got = [swap(h, w[0], "seq", count) for h, w in zip(hidden_held, ways)]
    ffn_gate_pre = times_right(ffn_input, ffn_gate)
    ffn_up_pre = times_right(ffn_input, ffn_up)
    grad_fgate, grad_fup = swish_back(ffn_gate_pre, ffn_up_pre, grad_fhidden)
    latent_chunks = [slice(j * latent_rows, (j + 1) * latent_rows) for j in chunks]

    def rows_home(mine):
        return tp_direct_sum([mine[rows] for rows in latent_chunks], tensor)

    post_sum = scatter_seq(times_plain(grad_fgate, ffn_gate) + times_plain(grad_fup, ffn_up))
    ffn_hidden = swish_gate(ffn_gate_pre, ffn_up_pre).astype(bf16)
    grad_ffn_down = times_left(ffn_hidden, cot_every)
    grad_ffn_gate = times_left(grad_fgate, ffn_input)
    grad_ffn_up = times_left(grad_fup, ffn_input)
    ffn_hidden_late = ffn_hidden
    if count == 8:
        ffn_hidden_late, *hidden_got = tie(ffn_hidden, *hidden_got)
    ffn_terms = times_plain(ffn_hidden_late, ffn_down).astype(bf16)
    post_sum, grad_ffn_down, grad_ffn_gate, grad_ffn_up, ffn_terms = tie(
        post_sum, grad_ffn_down, grad_ffn_gate, grad_ffn_up, ffn_terms
    )
    ffn_sum = scatter_seq(ffn_terms)
    grad_post = rows_home(post_sum)
    ignored, pull_post = jax.vjp(rms_norm, lat_after, post_gain)
    grad_lat_post, grad_post_gain = pull_post(grad_post)
    grad_after = cotangent.astype(f32) + grad_lat_post
    grad_after_all = jnp.concatenate(
        tp_direct([grad_after.astype(bf16)] * tensor, tensor), axis=0
    )
    grad_rmixed = (
        times_right(grad_after_all, ro_full)
        .astype(bf16)
        .reshape(latent_count, kv_local, group_size, HD_R)
    )
    grad_rq, grad_rk, grad_rv = attend_back(
        res_queries, res_keys, res_values, res_valid, res_scale, res_total, grad_rmixed
    )
    grad_kv = jnp.concatenate(
        [grad_rk.reshape(-1, kv_local * HD_R), grad_rv.reshape(-1, kv_local * HD_R)], axis=1
    )
    grad_kv_own = jnp.concatenate(
        tp_direct([rows_of(grad_kv, j) for j in chunks], tensor), axis=1
    )
    if count == 8:
        grad_kv_own, hidden_held, hidden_got = tie(grad_kv_own, hidden_held, hidden_got)
        hidden_far = [
            swap(h, w[1], "seq", count) for hs in (hidden_held, hidden_got) for h, w in zip(hs, ways)
        ]
    grad_ctx_norm = times_right(grad_kv_own, rkv_full)
    ignored, pull_ctx = jax.vjp(rms_norm, context, context_gain)
    grad_context, grad_context_gain = pull_ctx(grad_ctx_norm)

    grad_ctx = tp_gather(grad_context.astype(bf16), tensor)
    grad_rkv_ctx = scatter_seq(times_left(ctx_norm, grad_kv_own))
    both_every = gather_seq(jnp.concatenate([grad_after_all, res_mixed], axis=1))
    if count == 8:
        grad_ctx[2], *hidden_far[:2] = tie(grad_ctx[2], *hidden_far[:2])
    if count == 8:
        grad_ctx_turned = jnp.concatenate(grad_ctx, axis=0).T
        ctx_held = swap_each(
            lambda k: lax.dynamic_slice_in_dim(
                grad_ctx_turned, (seq_index ^ k) * own_cols, own_cols, 0
            ),
            count,
        )
    grad_pair, vis_parts = [], []
    steps = [chunks[i : i + 2] for i in range(0, tensor, 2)]
    for step in steps:
        rows = slice(step[0] * own_rows, (step[-1] + 1) * own_rows)
        grad_phidden = times_plain(
            jnp.concatenate([grad_ctx[j] for j in step], axis=0), pdown_full
        )
        grad_pair.append(
            jnp.concatenate(swish_back(gate_pre[rows], up_pre[rows], grad_phidden), axis=1)
        )
        if count == 8 and step is steps[-1]:
            grad_pair[-1], *ctx_held = tie(grad_pair[-1], *ctx_held)
        terms = times_right(grad_pair[-1], pair_full)
        vis_parts += [rows_of(terms, i) for i in range(len(step))]
    grad_vis = tp_direct_sum(vis_parts, tensor)
    grad_pair_sum = scatter_seq(times_left(vis_all, jnp.concatenate(grad_pair, axis=0)))
    grad_ctx_all = jnp.concatenate(grad_ctx, axis=0)

    grad_fc_out_rows = jnp.sum(grad_vis, axis=0)
    grad_vis, ffn_sum, grad_rkv_ctx, both_every = tie(grad_vis, ffn_sum, grad_rkv_ctx, both_every)
    if count == 8:
        grad_vis, *hidden_far[2:] = tie(grad_vis, *hidden_far[2:])
    grad_vis_rows = tp_gather(grad_vis.astype(bf16), tensor)
    grad_fc_pre = []
    for j in chunks:
        ignored, pull_gelu = jax.vjp(gelu_tanh, fc_pre[j])
        grad_fc_pre.append(pull_gelu(times_plain(grad_vis_rows[j], fc_out_full))[0].astype(bf16))
    grad_norm_two = tp_direct_sum([times_right(g, fc_in_full) for g in grad_fc_pre], tensor)
    grad_norm_two, grad_fc_late, grad_vis_late = tie(
        grad_norm_two, jnp.concatenate(grad_fc_pre, axis=0), jnp.concatenate(grad_vis_rows, axis=0)
    )
    if count == 8:
        hidden_held = hidden_held + hidden_got + hidden_far
        hidden_held = hidden_held + [swap(h, 1, "seq", count) for h in hidden_held]
    ignored, pull_two = jax.vjp(layer_norm, after_attn, mlp_norm_gain, mlp_norm_shift)
    grad_mid_norm, grad_mlp_gain, grad_mlp_shift = pull_two(grad_norm_two)
    grad_mid = grad_vis + grad_mid_norm
    grad_out_rows = jnp.sum(grad_mid, axis=0)
    grad_mid_all = jnp.concatenate(tp_gather(grad_mid.astype(bf16), tensor), axis=0)
    fc_in_sum = scatter_seq(times_left(jnp.concatenate(norm_two, axis=0), grad_fc_late))
    fc_out_sum = scatter_seq(times_left(grad_vis_late, jnp.concatenate(fc_act, axis=0)))
    grad_attended = (
        times_plain(grad_mid_all, out_full).astype(bf16).reshape(seq_len, vis_heads, 1, HD_V)
    )
    out_sum = scatter_seq(times_left(grad_mid_all, attended))
    grad_vq, grad_vk, grad_vv = attend_back(
        query_rows, key_rows, value_rows, vis_valid, vis_scale, vis_total, grad_attended
    )
    grad_qkv = jnp.concatenate(
        [g.reshape(seq_len, head_width) for g in (grad_vq, grad_vk, grad_vv)], axis=1
    )
    grad_lat_own = jnp.concatenate(
        [grad_rq.reshape(latent_count, query_width), grad_kv[seq_len:]], axis=1
    )
    grad_qkv, grad_lat_own, grad_rkv_ctx, ffn_sum, grad_pair_sum = tie(
        grad_qkv, grad_lat_own, grad_rkv_ctx, ffn_sum, grad_pair_sum
    )
    after_every = lax.dynamic_slice_in_dim(both_every, seq_index * own_cols, own_cols, 1)
    grad_res_out = times_left(both_every[:, d_text:], after_every)
    after_own = lax.dynamic_slice_in_dim(
        both_every[:, :d_text].reshape(count, latent_count, d_text),
        seq_index * own_cols,
        own_cols,
        2,
    )[:, :latent_rows]
    grad_after_sum = jnp.sum(after_own.astype(f32), axis=0)
    grad_lat_sum = jnp.sum(
        lax.all_gather(grad_lat_own, "seq", axis=0).astype(f32), axis=0
    )
    grad_lat_proj = grad_lat_sum.astype(bf16)
    grad_res = times_left(lat_norm_own, grad_lat_proj)
    grad_res_query = grad_res[:, :query_width]
    grad_lat_terms = jnp.concatenate(
        [
            times_right(grad_lat_proj, res_own),
            jnp.broadcast_to(
                jnp.sum(grad_lat_proj.astype(f32) * lat_proj_sum, axis=-1, keepdims=True),
                (latent_count, 128),
            ),
        ],
        axis=1,
    )
    lat_each = tp_direct([grad_lat_terms[rows] for rows in latent_chunks], tensor)
    grad_lat_norm = sum(lat_each[1:], lat_each[0])
    lat_inner = grad_lat_norm[:, own_cols : own_cols + 1] / lat_r
    grad_lat_norm = grad_lat_norm[:, :own_cols]
    grad_lat_rows = (
        lat_r * latent_gain_own * grad_lat_norm - lat_own * lat_r**3 * lat_inner / d_text
    )
    grad_latent_gain = jnp.sum(grad_lat_norm * lat_own * lat_r, axis=0)
    grad_latent_param = grad_lat_rows + grad_after_sum

    grad_rkv_ctx = tp_direct_sum(
        [grad_rkv_ctx[:, j * rkv_width : (j + 1) * rkv_width] for j in chunks], tensor
    )
    grad_rkv = grad_res[:, query_width:] + grad_rkv_ctx
    grad_res_key = grad_rkv[:, : kv_local * HD_R]
    grad_res_value = grad_rkv[:, kv_local * HD_R :]
    latents = (lat_after + rows_home(ffn_sum)).astype(bf16)
    if count == 8:
        grad_qkv, *hidden_held = tie(grad_qkv, *hidden_held)
        places = []
        for core in (0, 1):
            for step in (lambda w: 0, lambda w: w[0], lambda w: w[1], lambda w: w[0] ^ w[1]):
                places += [(step(w) ^ core, f) for f, w in enumerate(ways)]
        grad_proj_down = sum_of_products(ctx_held, hidden_held, places)
    else:
        grad_proj_down = scatter_seq(times_left(grad_ctx_all, hidden_all)).astype(f32)
    qkv_sum = scatter_seq(times_left(norm_all, grad_qkv))
    grad_norm_one = tp_scatter(lambda j: times_right(rows_of(grad_qkv, j), qkv_full), tensor)
    grad_fc_in_part = jnp.sum(grad_fc_late.astype(f32), axis=0)

    def sum_pieces(pieces):
        summed = sum_every(jnp.concatenate(pieces), tensor)
        sums, start = [], 0
        for piece in pieces:
            sums.append(summed[start : start + piece.shape[0]])
            start += piece.shape[0]
        return sums

    grad_norm_one, fc_in_sum, fc_out_sum = tie(grad_norm_one, fc_in_sum, fc_out_sum)
    grad_bias_part = jnp.sum(grad_qkv.astype(f32), axis=0)
    ignored, pull_one = jax.vjp(layer_norm, patch_rows, attn_norm_gain, attn_norm_shift)
    grad_in_norm, grad_attn_gain, grad_attn_shift = pull_one(grad_norm_one)
    patches_grad = grad_mid + grad_in_norm

    patches_grad, fc_in_sum, fc_out_sum, out_sum, qkv_sum = tie(
        patches_grad, fc_in_sum, fc_out_sum, out_sum, qkv_sum
    )
    grad_qkv_sum, grad_out = qkv_sum.astype(f32), out_sum.T.astype(f32)
    grad_fc_in, grad_fc_out = fc_in_sum.astype(f32), fc_out_sum.T.astype(f32)
    grad_proj_gate = grad_pair_sum[:, :proj_width].astype(f32)
    grad_proj_up = grad_pair_sum[:, proj_width:].astype(f32)

    late = sum_pieces(
        [
            grad_attn_gain,
            grad_attn_shift,
            spread_slot(grad_bias_part[:head_width], tensor, tp_index),
            spread_slot(grad_bias_part[2 * head_width :], tensor, tp_index),
            grad_out_rows,
            grad_mlp_gain,
            grad_mlp_shift,
            grad_fc_out_rows,
            spread_slot(grad_fc_in_part, tensor, tp_index),
            grad_context_gain,
            spread_slot(grad_latent_gain, count, seq_index),
            grad_post_gain,
        ]
    )
    sums = late[4:]
    return (
        latents,
        patches_grad,
        late[0],
        late[1],
        grad_qkv_sum[:, :head_width],
        take_slot(late[2], tensor, tp_index),
        grad_qkv_sum[:, head_width : 2 * head_width],
        grad_qkv_sum[:, 2 * head_width :],
        take_slot(late[3], tensor, tp_index),
        grad_out,
        sums[0],
        sums[1],
        sums[2],
        grad_fc_in,
        take_slot(sums[4], tensor, tp_index),
        grad_fc_out,
        sums[3],
        grad_proj_gate,
        grad_proj_up,
        grad_proj_down,
        grad_latent_param,
        sums[5],
        sums[6],
        grad_res_query,
        grad_res_key,
        grad_res_value,
        grad_res_out,
        sums[7],
        grad_ffn_gate,
        grad_ffn_up,
        grad_ffn_down,
    )


def solution(mesh):
    return jax.shard_map(
        shards,
        mesh=mesh,
        in_specs=(
            P(("seq", "tp"), None),
            P("seq"),
            P(),
            P(),
            P("seq", "tp"),
            P("tp"),
            P("seq", "tp"),
            P("seq", "tp"),
            P("tp"),
            P("tp", "seq"),
            P(),
            P(),
            P(),
            P("seq", "tp"),
            P("tp"),
            P("tp", "seq"),
            P(),
            P("seq", "tp"),
            P("seq", "tp"),
            P("seq", "tp"),
            P("tp", "seq"),
            P(),
            P(),
            P("seq", "tp"),
            P("seq", "tp"),
            P("seq", "tp"),
            P("tp", "seq"),
            P(),
            P(("seq", "tp"), None),
            P(("seq", "tp"), None),
            P(("seq", "tp"), None),
            P(("seq", "tp"), None),
        ),
        out_specs=(
            P(("seq", "tp"), None),
            P(("seq", "tp"), None),
            P(),
            P(),
            P("seq", "tp"),
            P("tp"),
            P("seq", "tp"),
            P("seq", "tp"),
            P("tp"),
            P("tp", "seq"),
            P(),
            P(),
            P(),
            P("seq", "tp"),
            P("tp"),
            P("tp", "seq"),
            P(),
            P("seq", "tp"),
            P("seq", "tp"),
            P("seq", "tp"),
            P("tp", "seq"),
            P(),
            P(),
            P("seq", "tp"),
            P("seq", "tp"),
            P("seq", "tp"),
            P("tp", "seq"),
            P(),
            P(("seq", "tp"), None),
            P(("seq", "tp"), None),
            P(("seq", "tp"), None),
        ),
        check_vma=False,
    )
```

time: 4240 us -> 1110 us (0.26)
  waiting for transfers between devices: 3560 us -> 483 us
  starting transfers between devices: 3.35 us -> 144 us
  matrix products: 412 us -> 283 us
  blocking collectives: 149 us -> 32.4 us
    reduce_scatter x28 -> x8, waiting for transfers between devices: 2580 us -> 2.07 us  [scatter_seq(): lax.psum_scatter(terms.astype(jnp.bfloat16), 'seq', scatter_dimension=axi...]
    all_gather x17 -> x7, waiting for transfers between devices: 971 us -> 95.4 us  [gather_seq(): return lax.all_gather(block, 'seq', axis=axis, tiled=True)]
    ppermute x0 -> x107, waiting for transfers between devices: none -> 384 us  [swap(): return lax.ppermute(value, axis, [(i, i ^ bit) for i in range(count)])]
    ppermute x0 -> x107, starting transfers between devices: none -> 142 us  [swap(): return lax.ppermute(value, axis, [(i, i ^ bit) for i in range(count)])]
    all_gather x11 -> x3, blocking collectives: 149 us -> 32.4 us  [the longest x1 12 us: shards(): lax.all_gather(grad_lat_own, 'seq', axis=0).astype(f32)]
    dot_general x16 -> x11, matrix products: 154 us -> 58.4 us  [times_left(): lax.dot_general(left_side, right_side, (((0,), (0,)), ((), ())), preferre...]
    dot_general x16 -> x19, matrix products: 124 us -> 99.8 us  [times_plain(): return jnp.dot(left_side, right_side, preferred_element_type=jnp.float32)]
    dot_general x16 -> x28, matrix products: 123 us -> 115 us  [times_right(): lax.dot_general(left_side, right_side, (((1,), (1,)), ((), ())), preferre...]
  transfers between devices with their start and end apart: 46 -> 122, of which waited for: 41 -> 57; matrix products, arithmetic and copies ran while one was open for 7% -> 32% of each run, Pallas kernels for 0% -> 2%
where the time goes in v1:
time: 1110 us; the launch traced here: 1100 us
  waiting for transfers between devices  483 us (44%)
  matrix products  283 us (25%)
  starting transfers between devices  144 us (13%)
  local copies, waits for them, and re-layouts  61.6 us (6%)
  other arithmetic  61.1 us (6%)
  blocking collectives  32.4 us (3%)
  Pallas kernels  20 us (2%)
  between operations  17.7 us (2%)
    ppermute x107, waiting for transfers between devices, swap(): return lax.ppermute(value, axis, [(i, i ^ bit) for i in range(count)])  384 us
    ppermute x107, starting transfers between devices, swap(): return lax.ppermute(value, axis, [(i, i ^ bit) for i in range(count)])  142 us
    dot_general x28, matrix products, times_right(): lax.dot_general(left_side, right_side, (((1,), (1,)), ((), ())), preferre...  115 us
    dot_general x19, matrix products, times_plain(): return jnp.dot(left_side, right_side, preferred_element_type=jnp.float32)  99.8 us
    all_gather x7, waiting for transfers between devices, gather_seq(): return lax.all_gather(block, 'seq', axis=axis, tiled=True)  95.4 us
    dot_general x11, matrix products, times_left(): lax.dot_general(left_side, right_side, (((0,), (0,)), ((), ())), preferre...  58.4 us
    unnamed x366, local copies, waits for them, and re-layouts  32 us
  transfers between devices with their start and end apart: 122, of which 57 were waited for; matrix products, arithmetic and copies ran while one was open for 32% of the time, Pallas kernels for 2%

profile of v1, /device:TPU:0, one launch (start us, length us, event | category | flops | bytes accessed | tf_op | source)
XLA Modules:
  0.0 1102.3 jit_solution(1754219290019969107)
XLA Ops:
  13.6 10.7 all_gather.33
  50.4 23.3 %collective-permute-done.1 = bf16[128,1152]{1,0:T(8,128)(2,1)} collective-permute-done((bf16[128,1152]{1,0:T(8,128)(2,1)S(1)}, bf16[128,1152]{1,0:T(8,128)(2,1)}, u32[]{:S(2)}, u32[]{:S(2)}) %collective-permute-start.1) | collective-permute-done | bytes 294944 | tf_op jit(solution)/shard_map/ppermute | solution.py:117
  75.4 8.6 collective-permute-done.8
  84.0 61.0 %all-gather.9.cloned.1.call-done = bf16[1152,10752]{1,0:T(8,128)(2,1)} async-done(((bf16[144,10752]{1,0:T(8,128)(2,1)}), bf16[1152,10752]{1,0:T(8,128)(2,1)}) %all-gather.9.cloned.1.call-update) | async-done | bytes 24772624 | tf_op jit(solution)/shard_map/all_gather | solution.py:166
  153.8 5.1 copy-done.65
  161.9 7.3 collective-permute-done.16
  172.6 7.0 collective-permute-done.15
  179.5 5.3 collective-permute-done.17
  190.0 9.4 collective-permute-done.20
  202.4 5.1 collective-permute-start.22
  211.7 5.9 collective-permute-done.22
  221.2 5.5 collective-permute-start.23
  232.7 9.6 collective-permute-start.25
  242.3 7.1 collective-permute-done.25
  256.1 16.5 %fusion.4 = f32[512,7168]{1,0:T(8,128)} fusion(bf16[1152,10752]{1,0:T(8,128)(2,1)} %all-gather.9.cloned.1.call-done, bf16[128,1152]{1,0:T(8,128)(2,1)S(1)} %collective-permute-done.26, bf16[128,1152]{1,0:T(8,128)(2,1)S(1)} %collective-permute-done.25, bf16[128,1152]{1,0:T(8,128)(2,1)S(1)} %collective-permute-done.24, bf16[128,1152]{1,0:T(8,128)(2,1)S(1)} %add_convert_fusion.2), kind=kOutput, calls=%fused_computation.5 | convolution fusion | flops 8460435456 | bytes 32374784 | tf_op jit(solution)/shard_map/dot_general | solution.py:52
  272.6 7.5 fusion.14
  281.4 8.7 all-gather.11.cloned.1.call-done
  290.1 8.3 fusion.61
  300.5 6.7 fusion.58
  309.4 6.4 fusion.55
  317.4 6.6 fusion.52
  332.6 13.7 %collective-permute-done.28 = bf16[128,1024]{0,1:T(8,128)(2,1)S(1)} collective-permute-done((bf16[128,1024]{0,1:T(8,128)(2,1)S(1)}, bf16[128,1024]{0,1:T(8,128)(2,1)S(1)}, u32[]{:S(2)}, u32[]{:S(2)}) %collective-permute-start.28) | collective-permute-done | bytes 262176 | tf_op jit(solution)/shard_map/ppermute | solution.py:117
  353.4 19.2 %collective-permute-done.35 = bf16[128,1024]{0,1:T(8,128)(2,1)S(1)} collective-permute-done((bf16[128,1024]{0,1:T(8,128)(2,1)S(1)}, bf16[128,1024]{0,1:T(8,128)(2,1)S(1)}, u32[]{:S(2)}, u32[]{:S(2)}) %collective-permute-start.35) | collective-permute-done | bytes 262176 | tf_op jit(solution)/shard_map/ppermute | solution.py:117
  372.7 5.5 collective-permute-done.32
  378.3 4.7 collective-permute-done.29
  383.7 7.2 convolution_convert_fusion.20
  412.6 4.4 collective-permute-done.43
  435.6 5.8 fusion.289
  441.4 25.6 %all-gather.19.cloned.1.call-done = bf16[512,4096]{1,0:T(8,128)(2,1)} async-done(((bf16[64,4096]{1,0:T(8,128)(2,1)}), bf16[512,4096]{1,0:T(8,128)(2,1)}) %all-gather.19.cloned.1.call-update) | async-done | bytes 4194320 | tf_op jit(solution)/shard_map/all_gather | solution.py:166
  467.0 6.0 fusion.290
  479.3 4.4 add_convert_fusion
  486.2 8.6 fusion.293
  494.8 5.8 fusion.294
  500.7 5.9 fusion.292
  506.6 31.0 %collective-permute-done.48.refs_10_ = bf16[256,3584]{1,0:T(8,128)(2,1)S(1)} collective-permute-done((bf16[256,3584]{1,0:T(8,128)(2,1)S(1)}, bf16[256,3584]{1,0:T(8,128)(2,1)S(1)}, u32[]{:S(2)}, u32[]{:S(2)}) %collective-permute-start.48) | collective-permute-done | bytes 1835040 | tf_op jit(solution)/shard_map/ppermute | solution.py:117
  556.0 6.3 collective-permute-done.51
  574.1 4.3 collective-permute-done.54
  595.1 6.9 multiply_reduce_fusion
  607.1 5.3 convolution_convert_fusion.3
  614.8 38.2 %collective-permute-done.61 = bf16[128,4096]{0,1:T(8,128)(2,1)} collective-permute-done((bf16[128,4096]{0,1:T(8,128)(2,1)S(1)}, bf16[128,4096]{0,1:T(8,128)(2,1)}, u32[]{:S(2)}, u32[]{:S(2)}) %collective-permute-start.61) | collective-permute-done | bytes 1048608 | tf_op jit(solution)/shard_map/ppermute | solution.py:117
  653.0 13.8 %fusion.44 = f32[256,3584]{1,0:T(8,128)S(1)} fusion(bf16[4096,3584]{1,0:T(8,128)(2,1)} %all-gather.11.cloned.1.call-done, bf16[128,4096]{0,1:T(8,128)(2,1)} %collective-permute-done.59, bf16[128,4096]{0,1:T(8,128)(2,1)S(1)} %fusion.42), kind=kOutput, calls=%fused_computation.86 | convolution fusion | flops 7520387072 | bytes 35127296 | tf_op jit(solution)/shard_map/dot_general | solution.py:52
  666.8 5.6 collective-permute-done.62.refs_12_
  682.8 21.0 %fusion.28 = (bf16[256,3584]{1,0:T(8,128)(2,1)}, bf16[256,3584]{1,0:T(8,128)(2,1)}, bf16[256,3584]{1,0:T(8,128)(2,1)}, bf16[256,3584]{1,0:T(8,128)(2,1)}) fusion(f32[256,3584]{1,0:T(8,128)S(1)} %fusion.44, f32[512,7168]{1,0:T(8,128)} %fusion.4, bf16[4096,3584]{1,0:T(8,128)(2,1)} %all-gather.11.cloned.1.call-done, ...), kind=kOutput, calls=%fused_computation.44 | convolution fusion | flops 7546077184 | bytes 57147392 | tf_op jit(solution)/shard_map/dot_general | solution.py:52
  710.9 8.8 collective-permute-done.67.refs_3_
  721.3 23.7 %collective-permute-done.69.refs_5_ = bf16[512,512]{1,0:T(8,128)(2,1)S(1)} collective-permute-done((bf16[512,512]{1,0:T(8,128)(2,1)}, bf16[512,512]{1,0:T(8,128)(2,1)S(1)}, u32[]{:S(2)}, u32[]{:S(2)}) %collective-permute-start.69) | collective-permute-done | bytes 524320 | tf_op jit(solution)/shard_map/ppermute | solution.py:117
  747.5 15.0 %convolution_convert_fusion = bf16[1152,7168]{1,0:T(8,128)(2,1)} fusion(bf16[256,7168]{1,0:T(8,128)(2,1)} %pad_maximum_fusion.1, bf16[256,3584]{1,0:T(8,128)(2,1)} %get-tuple-element.302, bf16[256,3584]{1,0:T(8,128)(2,1)} %get-tuple-element.301, bf16[128,1152]{1,0:T(8,128)(2,1)} %copy-done.164, bf16[128,1152]{1,0:T(8,128)(2,1)} %copy-done.162, ...), kind=kOutput, calls=%fused_computation | convolution fusion | flops 8490713088 | bytes 25034752 | tf_op jit(solution)/shard_map/dot_general | solution.py:56
  763.9 12.8 %fusion.2 = f32[256,1152]{1,0:T(8,128)} fusion(bf16[1152,10752]{1,0:T(8,128)(2,1)} %all-gather.9.cloned.1.call-done, bf16[256,3584]{1,0:T(8,128)(2,1)} %get-tuple-element.302, bf16[256,3584]{1,0:T(8,128)(2,1)} %get-tuple-element.301), kind=kOutput, calls=%fused_computation.3 | convolution fusion | flops 4235198464 | bytes 21364736 | tf_op jit(solution)/shard_map/dot_general | solution.py:62
  779.4 16.2 %fusion.35 = bf16[256,1152]{1,0:T(8,128)(2,1)} fusion(bf16[256,7168]{1,0:T(8,128)(2,1)} %pad_maximum_fusion.1, bf16[1152,10752]{1,0:T(8,128)(2,1)} %all-gather.9.cloned.1.call-done), kind=kOutput, calls=%fused_computation.61 | convolution fusion | flops 4228153344 | bytes 20774912 | tf_op jit(solution)/shard_map/dot_general | solution.py:62
  799.4 8.6 collective-permute-done.73
  808.1 18.1 %collective-permute-done.72 = bf16[128,1152]{1,0:T(8,128)(2,1)S(1)} collective-permute-done((bf16[128,1152]{1,0:T(8,128)(2,1)S(1)}, bf16[128,1152]{1,0:T(8,128)(2,1)S(1)}, u32[]{:S(2)}, u32[]{:S(2)}) %collective-permute-start.72) | collective-permute-done | bytes 294944 | tf_op jit(solution)/shard_map/ppermute | solution.py:117
  835.3 9.6 collective-permute-done.78
  860.3 7.0 collective-permute-done.80
  876.4 5.5 collective-permute-done.81
  888.8 4.9 convolution_convert_fusion.1
  901.6 6.1 collective-permute-start.83
  912.1 9.9 collective-permute-done.83
  927.8 5.2 collective-permute-done.84
  955.3 12.0 %all-gather = bf16[512,576]{1,0:T(8,128)(2,1)} all-gather(bf16[64,576]{1,0:T(8,128)(2,1)S(1)} %pad_maximum_fusion.22), channel_id=2, replica_groups=mesh['seq'=8,'tp'=4] {'seq'}, dimensions={0}, use_global_device_ids=true | all-gather | bytes 663552 | tf_op jit(solution)/shard_map/all_gather | solution.py:527
  995.9 20.0 %shard_map.543 = f32[512,3584]{1,0:T(8,128)} custom-call(bf16[512,512]{1,0:T(8,128)(2,1)S(1)} %get-tuple-element.158.refs_0_, bf16[512,512]{1,0:T(8,128)(2,1)S(1)} %collective-permute-done.65.refs_1_, bf16[512,512]{1,0:T(8,128)(2,1)S(1)} %collective-permute-done.66.refs_2_, bf16[512,512]{1,0:T(8,128)(2,1)S(1)} %copy-done.1, bf16[512,512]{1,0:T(8,128)(2,1)S(1)} %copy-done.3, ...), custom_call_target="tpu_custom_call" | custom-call | flops 15032385536 | bytes 36700160 | tf_op jit(solution)/shard_map/pallas_call | solution.py:190
  1030.3 10.9 collective-permute-done.97
  1048.3 10.5 collective-permute-done.104
  1066.0 4.7 collective-permute-done.102
  1072.6 4.4 collective-permute-done.103
  1076.9 9.7 all_gather.43
  (780 shorter events, 380.3 us)
Async XLA Ops:
  7.2 137.8 %all-gather.9.cloned.1.call-start = ((), (), s32[]{:S(2)}) async-start(), calls=%async_computation.8 | async-start | bytes 27869184 | tf_op jit(solution)/shard_map/all_gather | solution.py:166
  12.0 278.1 %all-gather.11.cloned.1.call-start = ((), (), s32[]{:S(2)}) async-start(), calls=%async_computation.9 | async-start | bytes 33030144 | tf_op jit(solution)/shard_map/all_gather | solution.py:166
  12.8 370.9 %all-gather.13.cloned.1.call-start = ((), (), s32[]{:S(2)}) async-start(), calls=%async_computation.10 | async-start | bytes 7077888 | tf_op jit(solution)/shard_map/all_gather | solution.py:166
  40.0 35.3 %collective-permute-start.10 = (bf16[512,192]{0,1:T(8,128)(2,1)S(1)}, bf16[512,192]{0,1:T(8,128)(2,1)S(1)}, u32[]{:S(2)}, u32[]{:S(2)}) collective-permute-start(bf16[512,192]{0,1:T(8,128)(2,1)S(1)} %get-tuple-element.378), channel_id=1, source_target_pairs={{0,2},{1,3},{2,0},{3,1},{4,6},{5,7},{6,4},{7,5},{8,10},{9,11},{10,... | collective-permute-start | bytes 589832 | tf_op jit(solution)/shard_map/ppermute | solution.py:117
  43.0 32.4 %collective-permute-start.11 = (bf16[512,192]{0,1:T(8,128)(2,1)S(1)}, bf16[512,192]{0,1:T(8,128)(2,1)S(1)}, u32[]{:S(2)}, u32[]{:S(2)}) collective-permute-start(bf16[512,192]{0,1:T(8,128)(2,1)S(1)} %get-tuple-element.378), channel_id=1, source_target_pairs={{0,3},{1,2},{2,1},{3,0},{4,7},{5,6},{6,5},{7,4},{8,11},{9,10},{10,... | collective-permute-start | bytes 589832 | tf_op jit(solution)/shard_map/ppermute | solution.py:117
  44.1 29.5 %collective-permute-start.1 = (bf16[128,1152]{1,0:T(8,128)(2,1)S(1)}, bf16[128,1152]{1,0:T(8,128)(2,1)}, u32[]{:S(2)}, u32[]{:S(2)}) collective-permute-start(bf16[128,1152]{1,0:T(8,128)(2,1)S(1)} %fusion.107), channel_id=1, source_target_pairs={{0,2},{1,3},{2,0},{3,1},{4,6},{5,7},{6,4},{7,5},{8,10},{9,11},{10,... | collective-permute-start | bytes 884744 | tf_op jit(solution)/shard_map/ppermute | solution.py:117
  45.6 28.1 %collective-permute-start.7 = (f32[64,576]{1,0:T(8,128)S(1)}, f32[64,576]{1,0:T(8,128)S(1)}, u32[]{:S(2)}, u32[]{:S(2)}) collective-permute-start(f32[64,576]{1,0:T(8,128)S(1)} %add.469), channel_id=1, source_target_pairs={{0,8},{4,12},{8,0},{12,4},{16,24},{20,28},{24,16},{28,20},{1,9},{5... | collective-permute-start | bytes 442376 | tf_op jit(solution)/shard_map/ppermute | solution.py:117
  50.4 94.6 %collective-permute-start = (bf16[128,1152]{1,0:T(8,128)(2,1)S(1)}, bf16[128,1152]{1,0:T(8,128)(2,1)S(1)}, u32[]{:S(2)}, u32[]{:S(2)}) collective-permute-start(bf16[128,1152]{1,0:T(8,128)(2,1)S(1)} %fusion.107), channel_id=1, source_target_pairs={{0,1},{1,0},{2,3},{3,2},{4,5},{5,4},{6,7},{7,6},{8,9},{9,8},{10,11... | collective-permute-start | bytes 884744 | tf_op jit(solution)/shard_map/ppermute | solution.py:117
  73.7 72.1 %collective-permute-start.2 = (bf16[128,1152]{1,0:T(8,128)(2,1)}, bf16[128,1152]{1,0:T(8,128)(2,1)}, u32[]{:S(2)}, u32[]{:S(2)}) collective-permute-start(bf16[128,1152]{1,0:T(8,128)(2,1)} %collective-permute-done.1), channel_id=1, source_target_pairs={{0,1},{1,0},{2,3},{3,2},{4,5},{5,4},{6,7},{7,6},{8,9},{9,8},{10,11... | collective-permute-start | bytes 884744 | tf_op jit(solution)/shard_map/ppermute | solution.py:117
  186.2 21.3 %collective-permute-start.18 = (bf16[128,1152]{1,0:T(8,128)(2,1)S(1)}, bf16[128,1152]{1,0:T(8,128)(2,1)S(1)}, u32[]{:S(2)}, u32[]{:S(2)}) collective-permute-start(bf16[128,1152]{1,0:T(8,128)(2,1)S(1)} %add_convert_fusion.3), channel_id=1, source_target_pairs={{0,1},{1,0},{2,3},{3,2},{4,5},{5,4},{6,7},{7,6},{8,9},{9,8},{10,11... | collective-permute-start | bytes 884744 | tf_op jit(solution)/shard_map/ppermute | solution.py:117
  202.4 26.3 %collective-permute-start.21 = (bf16[128,1152]{1,0:T(8,128)(2,1)S(1)}, bf16[128,1152]{1,0:T(8,128)(2,1)S(1)}, u32[]{:S(2)}, u32[]{:S(2)}) collective-permute-start(bf16[128,1152]{1,0:T(8,128)(2,1)S(1)} %convolution_convert_fusion.13), channel_id=1, source_target_pairs={{0,2},{1,3},{2,0},{3,1},{4,6},{5,7},{6,4},{7,5},{8,10},{9,11},{10,... | collective-permute-start | bytes 884744 | tf_op jit(solution)/shard_map/ppermute | solution.py:117
  280.2 121.5 %all-gather.15.cloned.1.call-start = ((), (), s32[]{:S(2)}) async-start(), calls=%async_computation.11 | async-start | bytes 3538944 | tf_op jit(solution)/shard_map/all_gather | solution.py:166
  280.8 137.5 %all-gather.17.cloned.1.call-start = ((), (), s32[]{:S(2)}) async-start(), calls=%async_computation.12 | async-start | bytes 4718592 | tf_op jit(solution)/shard_map/all_gather | solution.py:166
  281.4 185.6 %all-gather.19.cloned.1.call-start = ((), (), s32[]{:S(2)}) async-start(), calls=%async_computation.13 | async-start | bytes 4718592 | tf_op jit(solution)/shard_map/all_gather | solution.py:166
  298.4 25.6 %collective-permute-start.37 = (bf16[128,1024]{0,1:T(8,128)(2,1)S(1)}, bf16[128,1024]{0,1:T(8,128)(2,1)S(1)}, u32[]{:S(2)}, u32[]{:S(2)}) collective-permute-start(bf16[128,1024]{0,1:T(8,128)(2,1)S(1)} %get-tuple-element.329), channel_id=1, source_target_pairs={{0,1},{1,0},{2,3},{3,2},{4,5},{5,4},{6,7},{7,6},{8,9},{9,8},{10,11... | collective-permute-start | bytes 786440 | tf_op jit(solution)/shard_map/ppermute | solution.py:117
  300.0 47.8 %collective-permute-start.36 = (bf16[128,1024]{0,1:T(8,128)(2,1)S(1)}, bf16[128,1024]{0,1:T(8,128)(2,1)S(1)}, u32[]{:S(2)}, u32[]{:S(2)}) collective-permute-start(bf16[128,1024]{0,1:T(8,128)(2,1)S(1)} %get-tuple-element.328), channel_id=1, source_target_pairs={{0,1},{1,0},{2,3},{3,2},{4,5},{5,4},{6,7},{7,6},{8,9},{9,8},{10,11... | collective-permute-start | bytes 786440 | tf_op jit(solution)/shard_map/ppermute | solution.py:117
  308.8 41.6 %collective-permute-start.33 = (bf16[128,1024]{0,1:T(8,128)(2,1)S(1)}, bf16[128,1024]{0,1:T(8,128)(2,1)S(1)}, u32[]{:S(2)}, u32[]{:S(2)}) collective-permute-start(bf16[128,1024]{0,1:T(8,128)(2,1)S(1)} %get-tuple-element.326), channel_id=1, source_target_pairs={{0,1},{1,0},{2,3},{3,2},{4,5},{5,4},{6,7},{7,6},{8,9},{9,8},{10,11... | collective-permute-start | bytes 786440 | tf_op jit(solution)/shard_map/ppermute | solution.py:117
  324.1 48.6 %collective-permute-start.30 = (bf16[128,1024]{0,1:T(8,128)(2,1)S(1)}, bf16[128,1024]{0,1:T(8,128)(2,1)S(1)}, u32[]{:S(2)}, u32[]{:S(2)}) collective-permute-start(bf16[128,1024]{0,1:T(8,128)(2,1)S(1)} %get-tuple-element.324), channel_id=1, source_target_pairs={{0,1},{1,0},{2,3},{3,2},{4,5},{5,4},{6,7},{7,6},{8,9},{9,8},{10,11... | collective-permute-start | bytes 786440 | tf_op jit(solution)/shard_map/ppermute | solution.py:117
  325.3 21.0 %collective-permute-start.28 = (bf16[128,1024]{0,1:T(8,128)(2,1)S(1)}, bf16[128,1024]{0,1:T(8,128)(2,1)S(1)}, u32[]{:S(2)}, u32[]{:S(2)}) collective-permute-start(bf16[128,1024]{0,1:T(8,128)(2,1)S(1)} %get-tuple-element.323), channel_id=1, source_target_pairs={{0,1},{1,0},{2,3},{3,2},{4,5},{5,4},{6,7},{7,6},{8,9},{9,8},{10,11... | collective-permute-start | bytes 786440 | tf_op jit(solution)/shard_map/ppermute | solution.py:117
  346.3 26.3 %collective-permute-start.35 = (bf16[128,1024]{0,1:T(8,128)(2,1)S(1)}, bf16[128,1024]{0,1:T(8,128)(2,1)S(1)}, u32[]{:S(2)}, u32[]{:S(2)}) collective-permute-start(bf16[128,1024]{0,1:T(8,128)(2,1)S(1)} %add_convert_fusion.6), channel_id=1, source_target_pairs={{0,2},{1,3},{2,0},{3,1},{4,6},{5,7},{6,4},{7,5},{8,10},{9,11},{10,... | collective-permute-start | bytes 786440 | tf_op jit(solution)/shard_map/ppermute | solution.py:117
  347.8 30.5 %collective-permute-start.27 = (bf16[128,1024]{0,1:T(8,128)(2,1)S(1)}, bf16[128,1024]{0,1:T(8,128)(2,1)S(1)}, u32[]{:S(2)}, u32[]{:S(2)}) collective-permute-start(bf16[128,1024]{0,1:T(8,128)(2,1)S(1)} %get-tuple-element.322), channel_id=1, source_target_pairs={{0,1},{1,0},{2,3},{3,2},{4,5},{5,4},{6,7},{7,6},{8,9},{9,8},{10,11... | collective-permute-start | bytes 786440 | tf_op jit(solution)/shard_map/ppermute | solution.py:117
  350.3 27.9 %collective-permute-start.32 = (bf16[128,1024]{0,1:T(8,128)(2,1)S(1)}, bf16[128,1024]{0,1:T(8,128)(2,1)S(1)}, u32[]{:S(2)}, u32[]{:S(2)}) collective-permute-start(bf16[128,1024]{0,1:T(8,128)(2,1)S(1)} %add_convert_fusion.7), channel_id=1, source_target_pairs={{0,2},{1,3},{2,0},{3,1},{4,6},{5,7},{6,4},{7,5},{8,10},{9,11},{10,... | collective-permute-start | bytes 786440 | tf_op jit(solution)/shard_map/ppermute | solution.py:117
  350.4 32.5 %collective-permute-start.29 = (bf16[128,1024]{0,1:T(8,128)(2,1)S(1)}, bf16[128,1024]{0,1:T(8,128)(2,1)S(1)}, u32[]{:S(2)}, u32[]{:S(2)}) collective-permute-start(bf16[128,1024]{0,1:T(8,128)(2,1)S(1)} %add_convert_fusion.8), channel_id=1, source_target_pairs={{0,2},{1,3},{2,0},{3,1},{4,6},{5,7},{6,4},{7,5},{8,10},{9,11},{10,... | collective-permute-start | bytes 786440 | tf_op jit(solution)/shard_map/ppermute | solution.py:117
  431.6 114.9 %reduce-scatter.9.cloned.1.call-start = ((), (), s32[]{:S(2)}) async-start(), calls=%async_computation.14 | async-start | bytes 4718592 | tf_op jit(solution)/shard_map/reduce_scatter | solution.py:170
  483.6 345.3 %reduce-scatter.11.cloned.1.call-start = ((), (), s32[]{:S(2)}) async-start(), calls=%async_computation.15 | async-start | bytes 4718592 | tf_op jit(solution)/shard_map/reduce_scatter | solution.py:170
  484.1 53.5 %collective-permute-start.48 = (bf16[256,3584]{1,0:T(8,128)(2,1)S(1)}, bf16[256,3584]{1,0:T(8,128)(2,1)S(1)}, u32[]{:S(2)}, u32[]{:S(2)}) collective-permute-start(bf16[256,3584]{1,0:T(8,128)(2,1)S(1)} %get-tuple-element.166.refs_8_), channel_id=1, source_target_pairs={{0,8},{4,12},{8,0},{12,4},{16,24},{20,28},{24,16},{28,20},{1,9},{5... | collective-permute-start | bytes 5505032 | tf_op jit(solution)/shard_map/ppermute | solution.py:117
  485.6 53.3 %collective-permute-start.49 = (bf16[256,3584]{1,0:T(8,128)(2,1)}, bf16[256,3584]{1,0:T(8,128)(2,1)S(1)}, u32[]{:S(2)}, u32[]{:S(2)}) collective-permute-start(bf16[256,3584]{1,0:T(8,128)(2,1)} %get-tuple-element.167.refs_9_), channel_id=1, source_target_pairs={{0,16},{4,20},{8,24},{12,28},{16,0},{20,4},{24,8},{28,12},{1,17},{... | collective-permute-start | bytes 5505032 | tf_op jit(solution)/shard_map/ppermute | solution.py:117
  546.5 282.4 %all-gather.21.cloned.1.call-start = ((), (), s32[]{:S(2)}) async-start(), calls=%async_computation.17 | async-start | bytes 5160960 | tf_op jit(solution)/shard_map/all_gather | solution.py:166
  581.4 247.6 %reduce-scatter.13.cloned.1.call-start = ((), (), s32[]{:S(2)}) async-start(), calls=%async_computation.16 | async-start | bytes 7077888 | tf_op jit(solution)/shard_map/reduce_scatter | solution.py:170
  604.4 48.6 %collective-permute-start.59 = (bf16[128,4096]{0,1:T(8,128)(2,1)S(1)}, bf16[128,4096]{0,1:T(8,128)(2,1)}, u32[]{:S(2)}, u32[]{:S(2)}) collective-permute-start(bf16[128,4096]{0,1:T(8,128)(2,1)S(1)} %fusion.42), channel_id=1, source_target_pairs={{0,1},{1,0},{2,3},{3,2},{4,5},{5,4},{6,7},{7,6},{8,9},{9,8},{10,11... | collective-permute-start | bytes 3145736 | tf_op jit(solution)/shard_map/ppermute | solution.py:117
  605.6 47.3 %collective-permute-start.61 = (bf16[128,4096]{0,1:T(8,128)(2,1)S(1)}, bf16[128,4096]{0,1:T(8,128)(2,1)}, u32[]{:S(2)}, u32[]{:S(2)}) collective-permute-start(bf16[128,4096]{0,1:T(8,128)(2,1)S(1)} %fusion.42), channel_id=1, source_target_pairs={{0,2},{1,3},{2,0},{3,1},{4,6},{5,7},{6,4},{7,5},{8,10},{9,11},{10,... | collective-permute-start | bytes 3145736 | tf_op jit(solution)/shard_map/ppermute | solution.py:117
  612.4 334.9 %reduce-scatter.15.cloned.1.call-start = ((), (), s32[]{:S(2)}) async-start(), calls=%async_computation.18 | async-start | bytes 18579456 | tf_op jit(solution)/shard_map/reduce_scatter | solution.py:170
  612.6 59.8 %collective-permute-start.62 = (bf16[256,3584]{1,0:T(8,128)(2,1)S(1)}, bf16[256,3584]{1,0:T(8,128)(2,1)}, u32[]{:S(2)}, u32[]{:S(2)}) collective-permute-start(bf16[256,3584]{1,0:T(8,128)(2,1)S(1)} %get-tuple-element.166.refs_8_), channel_id=1, source_target_pairs={{0,16},{4,20},{8,24},{12,28},{16,0},{20,4},{24,8},{28,12},{1,17},{... | collective-permute-start | bytes 5505032 | tf_op jit(solution)/shard_map/ppermute | solution.py:117
  614.1 58.4 %collective-permute-start.63 = (bf16[256,3584]{1,0:T(8,128)(2,1)}, bf16[256,3584]{1,0:T(8,128)(2,1)}, u32[]{:S(2)}, u32[]{:S(2)}) collective-permute-start(bf16[256,3584]{1,0:T(8,128)(2,1)} %get-tuple-element.167.refs_9_), channel_id=1, source_target_pairs={{0,8},{4,12},{8,0},{12,4},{16,24},{20,28},{24,16},{28,20},{1,9},{5... | collective-permute-start | bytes 5505032 | tf_op jit(solution)/shard_map/ppermute | solution.py:117
  653.0 22.3 %collective-permute-start.64 = (bf16[128,4096]{0,1:T(8,128)(2,1)}, bf16[128,4096]{0,1:T(8,128)(2,1)S(1)}, u32[]{:S(2)}, u32[]{:S(2)}) collective-permute-start(bf16[128,4096]{0,1:T(8,128)(2,1)} %collective-permute-done.61), channel_id=1, source_target_pairs={{0,1},{1,0},{2,3},{3,2},{4,5},{5,4},{6,7},{7,6},{8,9},{9,8},{10,11... | collective-permute-start | bytes 3145736 | tf_op jit(solution)/shard_map/ppermute | solution.py:117
  679.3 24.5 %collective-permute-start.65 = (bf16[512,512]{1,0:T(8,128)(2,1)}, bf16[512,512]{1,0:T(8,128)(2,1)S(1)}, u32[]{:S(2)}, u32[]{:S(2)}) collective-permute-start(bf16[512,512]{1,0:T(8,128)(2,1)} %get-tuple-element.313), channel_id=1, source_target_pairs={{0,4},{4,0},{8,12},{12,8},{16,20},{20,16},{24,28},{28,24},{1,5},{5... | collective-permute-start | bytes 1572872 | tf_op jit(solution)/shard_map/ppermute | solution.py:117
  679.3 26.1 %collective-permute-start.66 = (bf16[512,512]{1,0:T(8,128)(2,1)}, bf16[512,512]{1,0:T(8,128)(2,1)S(1)}, u32[]{:S(2)}, u32[]{:S(2)}) collective-permute-start(bf16[512,512]{1,0:T(8,128)(2,1)} %get-tuple-element.312), channel_id=1, source_target_pairs={{0,8},{4,12},{8,0},{12,4},{16,24},{20,28},{24,16},{28,20},{1,9},{5... | collective-permute-start | bytes 1572872 | tf_op jit(solution)/shard_map/ppermute | solution.py:117
  680.7 39.0 %collective-permute-start.67 = (bf16[512,512]{1,0:T(8,128)(2,1)}, bf16[512,512]{1,0:T(8,128)(2,1)S(1)}, u32[]{:S(2)}, u32[]{:S(2)}) collective-permute-start(bf16[512,512]{1,0:T(8,128)(2,1)} %get-tuple-element.311), channel_id=1, source_target_pairs={{0,12},{4,8},{8,4},{12,0},{16,28},{20,24},{24,20},{28,16},{1,13},{... | collective-permute-start | bytes 1572872 | tf_op jit(solution)/shard_map/ppermute | solution.py:117
  681.2 39.3 %collective-permute-start.68 = (bf16[512,512]{1,0:T(8,128)(2,1)}, bf16[512,512]{1,0:T(8,128)(2,1)S(1)}, u32[]{:S(2)}, u32[]{:S(2)}) collective-permute-start(bf16[512,512]{1,0:T(8,128)(2,1)} %get-tuple-element.310), channel_id=1, source_target_pairs={{0,16},{4,20},{8,24},{12,28},{16,0},{20,4},{24,8},{28,12},{1,17},{... | collective-permute-start | bytes 1572872 | tf_op jit(solution)/shard_map/ppermute | solution.py:117
  682.5 62.5 %collective-permute-start.69 = (bf16[512,512]{1,0:T(8,128)(2,1)}, bf16[512,512]{1,0:T(8,128)(2,1)S(1)}, u32[]{:S(2)}, u32[]{:S(2)}) collective-permute-start(bf16[512,512]{1,0:T(8,128)(2,1)} %get-tuple-element.309), channel_id=1, source_target_pairs={{0,20},{4,16},{8,28},{12,24},{16,4},{20,0},{24,12},{28,8},{1,21},{... | collective-permute-start | bytes 1572872 | tf_op jit(solution)/shard_map/ppermute | solution.py:117
  703.8 42.0 %collective-permute-start.70 = (bf16[512,512]{1,0:T(8,128)(2,1)}, bf16[512,512]{1,0:T(8,128)(2,1)S(1)}, u32[]{:S(2)}, u32[]{:S(2)}) collective-permute-start(bf16[512,512]{1,0:T(8,128)(2,1)} %get-tuple-element.308), channel_id=1, source_target_pairs={{0,24},{4,28},{8,16},{12,20},{16,8},{20,12},{24,0},{28,4},{1,25},{... | collective-permute-start | bytes 1572872 | tf_op jit(solution)/shard_map/ppermute | solution.py:117
  705.4 41.3 %collective-permute-start.71 = (bf16[512,512]{1,0:T(8,128)(2,1)}, bf16[512,512]{1,0:T(8,128)(2,1)S(1)}, u32[]{:S(2)}, u32[]{:S(2)}) collective-permute-start(bf16[512,512]{1,0:T(8,128)(2,1)} %get-tuple-element.307), channel_id=1, source_target_pairs={{0,28},{4,24},{8,20},{12,16},{16,12},{20,8},{24,4},{28,0},{1,29},{... | collective-permute-start | bytes 1572872 | tf_op jit(solution)/shard_map/ppermute | solution.py:117
  762.4 301.9 %reduce-scatter.17.cloned.1.call-start = ((), (), s32[]{:S(2)}) async-start(), calls=%async_computation.19 | async-start | bytes 2985984 | tf_op jit(solution)/shard_map/reduce_scatter | solution.py:170
  762.9 66.1 %collective-permute-start.74 = (bf16[256,3584]{1,0:T(8,128)(2,1)}, bf16[256,3584]{1,0:T(8,128)(2,1)}, u32[]{:S(2)}, u32[]{:S(2)}) collective-permute-start(bf16[256,3584]{1,0:T(8,128)(2,1)} %copy-done.151), channel_id=1, source_target_pairs={{0,16},{4,20},{8,24},{12,28},{16,0},{20,4},{24,8},{28,12},{1,17},{... | collective-permute-start | bytes 5505032 | tf_op jit(solution)/shard_map/ppermute | solution.py:117
  763.0 66.0 %collective-permute-start.75 = (bf16[256,3584]{1,0:T(8,128)(2,1)}, bf16[256,3584]{1,0:T(8,128)(2,1)}, u32[]{:S(2)}, u32[]{:S(2)}) collective-permute-start(bf16[256,3584]{1,0:T(8,128)(2,1)} %copy-done.152), channel_id=1, source_target_pairs={{0,8},{4,12},{8,0},{12,4},{16,24},{20,28},{24,16},{28,20},{1,9},{5... | collective-permute-start | bytes 5505032 | tf_op jit(solution)/shard_map/ppermute | solution.py:117
  797.9 28.2 %collective-permute-start.72 = (bf16[128,1152]{1,0:T(8,128)(2,1)S(1)}, bf16[128,1152]{1,0:T(8,128)(2,1)S(1)}, u32[]{:S(2)}, u32[]{:S(2)}) collective-permute-start(bf16[128,1152]{1,0:T(8,128)(2,1)S(1)} %get-tuple-element.336), channel_id=1, source_target_pairs={{0,2},{1,3},{2,0},{3,1},{4,6},{5,7},{6,4},{7,5},{8,10},{9,11},{10,... | collective-permute-start | bytes 884744 | tf_op jit(solution)/shard_map/ppermute | solution.py:117
  830.2 24.0 %collective-permute-start.76 = (bf16[128,1152]{1,0:T(8,128)(2,1)S(1)}, bf16[128,1152]{1,0:T(8,128)(2,1)S(1)}, u32[]{:S(2)}, u32[]{:S(2)}) collective-permute-start(bf16[128,1152]{1,0:T(8,128)(2,1)S(1)} %convert_element_type.571), channel_id=1, source_target_pairs={{0,1},{1,0},{2,3},{3,2},{4,5},{5,4},{6,7},{7,6},{8,9},{9,8},{10,11... | collective-permute-start | bytes 884744 | tf_op jit(solution)/shard_map/ppermute | solution.py:117
  851.1 25.3 %collective-permute-start.79 = (bf16[128,1152]{1,0:T(8,128)(2,1)S(1)}, bf16[128,1152]{1,0:T(8,128)(2,1)S(1)}, u32[]{:S(2)}, u32[]{:S(2)}) collective-permute-start(bf16[128,1152]{1,0:T(8,128)(2,1)S(1)} %convolution_convert_fusion.10), channel_id=1, source_target_pairs={{0,2},{1,3},{2,0},{3,1},{4,6},{5,7},{6,4},{7,5},{8,10},{9,11},{10,... | collective-permute-start | bytes 884744 | tf_op jit(solution)/shard_map/ppermute | solution.py:117
  888.8 175.6 %reduce-scatter.19.cloned.1.call-start = ((), (), s32[]{:S(2)}) async-start(), calls=%async_computation.20 | async-start | bytes 2985984 | tf_op jit(solution)/shard_map/reduce_scatter | solution.py:170
  893.7 196.2 %reduce-scatter.21.cloned.1.call-start = ((), (), s32[]{:S(2)}) async-start(), calls=%async_computation.21 | async-start | bytes 995328 | tf_op jit(solution)/shard_map/reduce_scatter | solution.py:170
  895.0 43.4 %collective-permute-start.88 = (bf16[256,3584]{1,0:T(8,128)(2,1)S(1)}, bf16[256,3584]{1,0:T(8,128)(2,1)}, u32[]{:S(2)}, u32[]{:S(2)}) collective-permute-start(bf16[256,3584]{1,0:T(8,128)(2,1)S(1)} %get-tuple-element.166.refs_8_), channel_id=1, source_target_pairs={{0,4},{4,0},{8,12},{12,8},{16,20},{20,16},{24,28},{28,24},{1,5},{5... | collective-permute-start | bytes 5505032 | tf_op jit(solution)/shard_map/ppermute | solution.py:117
  895.0 44.0 %collective-permute-start.89 = (bf16[256,3584]{1,0:T(8,128)(2,1)}, bf16[256,3584]{1,0:T(8,128)(2,1)}, u32[]{:S(2)}, u32[]{:S(2)}) collective-permute-start(bf16[256,3584]{1,0:T(8,128)(2,1)} %get-tuple-element.167.refs_9_), channel_id=1, source_target_pairs={{0,4},{4,0},{8,12},{12,8},{16,20},{20,16},{24,28},{28,24},{1,5},{5... | collective-permute-start | bytes 5505032 | tf_op jit(solution)/shard_map/ppermute | solution.py:117
  895.5 43.6 %collective-permute-start.90 = (bf16[256,3584]{1,0:T(8,128)(2,1)}, bf16[256,3584]{1,0:T(8,128)(2,1)}, u32[]{:S(2)}, u32[]{:S(2)}) collective-permute-start(bf16[256,3584]{1,0:T(8,128)(2,1)} %copy-done.151), channel_id=1, source_target_pairs={{0,4},{4,0},{8,12},{12,8},{16,20},{20,16},{24,28},{28,24},{1,5},{5... | collective-permute-start | bytes 5505032 | tf_op jit(solution)/shard_map/ppermute | solution.py:117
  936.0 153.9 %reduce-scatter.23.cloned.1.call-start = ((), (), s32[]{:S(2)}) async-start(), calls=%async_computation.22 | async-start | bytes 2322432 | tf_op jit(solution)/shard_map/reduce_scatter | solution.py:170
  973.1 51.0 %collective-permute-start.87 = (bf16[16,4096]{1,0:T(8,128)(2,1)}, bf16[16,4096]{1,0:T(8,128)(2,1)}, u32[]{:S(2)}, u32[]{:S(2)}) collective-permute-start(bf16[16,4096]{1,0:T(8,128)(2,1)} %get-tuple-element.341), channel_id=1, source_target_pairs={{0,3},{1,2},{2,1},{3,0},{4,7},{5,6},{6,5},{7,4},{8,11},{9,10},{10,... | collective-permute-start | bytes 393224 | tf_op jit(solution)/shard_map/ppermute | solution.py:117
  973.1 52.1 %collective-permute-start.86 = (bf16[16,4096]{1,0:T(8,128)(2,1)}, bf16[16,4096]{1,0:T(8,128)(2,1)}, u32[]{:S(2)}, u32[]{:S(2)}) collective-permute-start(bf16[16,4096]{1,0:T(8,128)(2,1)} %get-tuple-element.342), channel_id=1, source_target_pairs={{0,2},{1,3},{2,0},{3,1},{4,6},{5,7},{6,4},{7,5},{8,10},{9,11},{10,... | collective-permute-start | bytes 393224 | tf_op jit(solution)/shard_map/ppermute | solution.py:117
  974.6 43.5 %collective-permute-start.101 = (f32[16,640]{1,0:T(8,128)}, f32[16,640]{1,0:T(8,128)}, u32[]{:S(2)}, u32[]{:S(2)}) collective-permute-start(f32[16,640]{1,0:T(8,128)} %get-tuple-element.365), channel_id=1, source_target_pairs={{0,3},{1,2},{2,1},{3,0},{4,7},{5,6},{6,5},{7,4},{8,11},{9,10},{10,... | collective-permute-start | bytes 122888 | tf_op jit(solution)/shard_map/ppermute | solution.py:117
  977.6 42.5 %collective-permute-start.100 = (f32[16,640]{1,0:T(8,128)}, f32[16,640]{1,0:T(8,128)}, u32[]{:S(2)}, u32[]{:S(2)}) collective-permute-start(f32[16,640]{1,0:T(8,128)} %get-tuple-element.366), channel_id=1, source_target_pairs={{0,2},{1,3},{2,0},{3,1},{4,6},{5,7},{6,4},{7,5},{8,10},{9,11},{10,... | collective-permute-start | bytes 122888 | tf_op jit(solution)/shard_map/ppermute | solution.py:117
  979.7 40.6 %collective-permute-start.99 = (f32[16,640]{1,0:T(8,128)}, f32[16,640]{1,0:T(8,128)}, u32[]{:S(2)}, u32[]{:S(2)}) collective-permute-start(f32[16,640]{1,0:T(8,128)} %get-tuple-element.364), channel_id=1, source_target_pairs={{0,1},{1,0},{2,3},{3,2},{4,5},{5,4},{6,7},{7,6},{8,9},{9,8},{10,11... | collective-permute-start | bytes 122888 | tf_op jit(solution)/shard_map/ppermute | solution.py:117
  1020.2 21.0 %collective-permute-start.97 = (bf16[128,1152]{1,0:T(8,128)(2,1)}, bf16[128,1152]{1,0:T(8,128)(2,1)S(1)}, u32[]{:S(2)}, u32[]{:S(2)}) collective-permute-start(bf16[128,1152]{1,0:T(8,128)(2,1)} %convolution_convert_fusion.7), channel_id=1, source_target_pairs={{0,1},{1,0},{2,3},{3,2},{4,5},{5,4},{6,7},{7,6},{8,9},{9,8},{10,11... | collective-permute-start | bytes 884744 | tf_op jit(solution)/shard_map/ppermute | solution.py:117
  1020.3 41.5 %collective-permute-start.96 = (bf16[128,1152]{1,0:T(8,128)(2,1)}, bf16[128,1152]{1,0:T(8,128)(2,1)}, u32[]{:S(2)}, u32[]{:S(2)}) collective-permute-start(bf16[128,1152]{1,0:T(8,128)(2,1)} %convolution_convert_fusion.8), channel_id=1, source_target_pairs={{0,1},{1,0},{2,3},{3,2},{4,5},{5,4},{6,7},{7,6},{8,9},{9,8},{10,11... | collective-permute-start | bytes 884744 | tf_op jit(solution)/shard_map/ppermute | solution.py:117
  1024.1 22.2 %collective-permute-start.106 = (bf16[512,192]{1,0:T(8,128)(2,1)S(1)}, bf16[512,192]{1,0:T(8,128)(2,1)S(1)}, u32[]{:S(2)}, u32[]{:S(2)}) collective-permute-start(bf16[512,192]{1,0:T(8,128)(2,1)S(1)} %copy-done.78), channel_id=1, source_target_pairs={{0,3},{1,2},{2,1},{3,0},{4,7},{5,6},{6,5},{7,4},{8,11},{9,10},{10,... | collective-permute-start | bytes 589832 | tf_op jit(solution)/shard_map/ppermute | solution.py:117
  1025.2 23.0 %collective-permute-start.105 = (bf16[512,192]{1,0:T(8,128)(2,1)S(1)}, bf16[512,192]{1,0:T(8,128)(2,1)S(1)}, u32[]{:S(2)}, u32[]{:S(2)}) collective-permute-start(bf16[512,192]{1,0:T(8,128)(2,1)S(1)} %copy-done.77), channel_id=1, source_target_pairs={{0,2},{1,3},{2,0},{3,1},{4,6},{5,7},{6,4},{7,5},{8,10},{9,11},{10,... | collective-permute-start | bytes 589832 | tf_op jit(solution)/shard_map/ppermute | solution.py:117
  1025.7 33.1 %collective-permute-start.104 = (bf16[512,192]{1,0:T(8,128)(2,1)S(1)}, bf16[512,192]{1,0:T(8,128)(2,1)S(1)}, u32[]{:S(2)}, u32[]{:S(2)}) collective-permute-start(bf16[512,192]{1,0:T(8,128)(2,1)S(1)} %copy-done.76), channel_id=1, source_target_pairs={{0,1},{1,0},{2,3},{3,2},{4,5},{5,4},{6,7},{7,6},{8,9},{9,8},{10,11... | collective-permute-start | bytes 589832 | tf_op jit(solution)/shard_map/ppermute | solution.py:117
  (234 other events, 3258.0 us)
Sparse Core Ops, SparseCore 0:
  12.0 132.9 all-gather.8
  146.9 143.0 all-gather.10
  292.5 46.6 all-gather.12
  340.9 32.8 all-gather.14
  376.1 36.7 all-gather.16
  431.7 35.2 all-gather.18
  483.8 62.7 reduce-scatter.8
  550.2 51.3 reduce-scatter.10
  604.1 56.9 all-gather.20
  664.9 98.7 reduce-scatter.12
  767.9 114.7 reduce-scatter.14
  888.9 50.9 reduce-scatter.16
  943.8 43.7 reduce-scatter.18
  990.7 35.1 reduce-scatter.20
  1029.4 40.8 reduce-scatter.22
